TPU v7x, 32 devices: a whole 2x2x4 slice. The times are simulated.
32 devices in a mesh: runs: 2 (over x), gy: 16 (over z, y, core).
Axes of the slice: x: 2, y: 2, z: 4, core: 2. Of those that a mesh axis runs over, the one named last changes fastest.
Arguments:
- depth: float32 [1024, 1920], P(('runs', 'gy')), parts along dimension 0, may hold values from 0.02 to 3
- flux_east: float32 [1024, 1920], P(('runs', 'gy')), parts along dimension 0, may hold values from -2 to 2
- flux_south: float32 [1024, 1920], P(('runs', 'gy')), parts along dimension 0, may hold values from -2 to 2
- river_section: float32 [4096], P(('runs', 'gy')), parts along dimension 0, may hold values from 0 to 2
- bed_level: float32 [512, 1920], P('gy'), may hold values from -3 to 3
- rough_class: int32 [512, 1920], P('gy'), may hold values from 0 to 7
- manning_table: float32 [8], replicated, may hold values from 0.02 to 0.15
- bank_cell: int32 [4, 2048], P(None, 'gy'), may hold values from 0 to 983039, as said below
Outputs:
- depth_out: float32 [1024, 1920], P(('runs', 'gy')), parts along dimension 0
- east_out: float32 [1024, 1920], P(('runs', 'gy')), parts along dimension 0
- south_out: float32 [1024, 1920], P(('runs', 'gy')), parts along dimension 0
- section_out: float32 [4096], P(('runs', 'gy')), parts along dimension 0
There are 2 independent parts, one for each index of `runs`. A program takes and returns all parts, laid end to end along the dimension named above; an argument that names none is the same for every part. Nothing has to cross between parts.
Inputs may be any that keep to these rules, and one draw needn't show every extreme that they name: `bank_cell`: the 4 corridor cells of a node are consecutive flat indices row * 1920 + column within one map row. Node n is owned by gy index o = n // 128, and all its corridor cells lie in map rows from max((o - 1) * 32, 0) to min((o + 2) * 32, 512) - 1.
All inputs are finite; a program needn't handle non-finite values.
Results may differ from a plain program's by a relative error of at most 0.00013.
Values sent between devices are 32-bit elements; how exact they have to be, the bound alone decides.
No kernel may reach another device: no remote copies, remote signals or barrier semaphores. Data moves between devices by JAX's collectives and lax.ppermute only.
A program may use at most 64 MiB of HBM per device.

v0:
```python
import functools

import jax
import jax.numpy as jnp
from jax import lax
from jax.experimental import pallas as pl
from jax.experimental.pallas import tpu as pltpu
from jax.sharding import PartitionSpec as P

STEPS = 4

GRAV = 9.81
TSTEP = 8.0
CELL = 90.0
FLOOR = 0.05
BANK_COEF = 200.0
CELL_AREA = 8100.0
NODE_AREA = 20000.0

LANES = 128
HALO = 4
SLOPE = GRAV * TSTEP / CELL
SPREAD = TSTEP / CELL
FEED = TSTEP * BANK_COEF / CELL_AREA
DRAIN = TSTEP * BANK_COEF / NODE_AREA
VMEM_LIMIT = 32 * 1024 * 1024

SMEM_SPEC = pl.BlockSpec(memory_space=pltpu.SMEM)
VMEM_SPEC = pl.BlockSpec(memory_space=pltpu.VMEM)
HBM_SPEC = pl.BlockSpec(memory_space=pltpu.HBM)


def swapped(value, first):
    count = lax.axis_size("gy")
    pairs = []
    for low in range(first, count - 1, 2):
        pairs += [(low, low + 1), (low + 1, low)]
    return lax.ppermute(value, "gy", pairs)


def cols(chunk):
    return slice(chunk * LANES, (chunk + 1) * LANES)


def lanes_of(rows):
    return lax.broadcasted_iota(jnp.int32, (rows, LANES), 1)


def moved_left(value, following, by):
    return jnp.where(
        lanes_of(value.shape[0]) >= LANES - by,
        pltpu.roll(following, LANES - by, 1),
        pltpu.roll(value, LANES - by, 1),
    )


def moved_up(value):
    return pltpu.roll(value, value.shape[0] - 1, 0)


def split3(value):
    high = value.astype(jnp.bfloat16)
    rest = value - high.astype(jnp.float32)
    middle = rest.astype(jnp.bfloat16)
    low = (rest - middle.astype(jnp.float32)).astype(jnp.bfloat16)
    return high, middle, low


def one_hot(count, key):
    rows = lax.broadcasted_iota(jnp.int32, (count, key.shape[1]), 0)
    return jnp.where(rows == key, 1.0, 0.0)


def drag_of(mann_a, mann_b):
    pair = mann_a + mann_b
    return (0.25 * GRAV * TSTEP) * (pair * pair)


def looked_up(klass, entries):
    value = jnp.broadcast_to(entries[0], klass.shape)
    for k in range(1, len(entries)):
        value = jnp.where(klass == k, entries[k], value)
    return value


def face(flux, surf_a, surf_b, bed_max, drag):
    flow_depth = jnp.maximum(jnp.maximum(surf_a, surf_b) - bed_max, FLOOR)
    power = jnp.exp2((-7.0 / 3.0) * jnp.log2(flow_depth))
    driven = flux - SLOPE * flow_depth * (surf_b - surf_a)
    damping = 1.0 + drag * jnp.abs(flux) * power
    return driven * pl.reciprocal(damping, approx=True)


def right_sum(value, state):
    lane = lanes_of(value.shape[0])
    once = pltpu.roll(value, 1, 1)
    pair = value + jnp.where(lane < 1, state[0], once)
    twice = pltpu.roll(pair, 2, 1)
    return pair + jnp.where(lane < 2, state[1], twice), (once, twice)


def east_walled(value, chunk, chunks):
    if chunk + 1 < chunks:
        return value
    return jnp.where(lanes_of(value.shape[0]) == LANES - 1, 0.0, value)


def located(cell, position, rows, ext, columns):
    base = ((position * rows - HALO) * columns + 1).astype(jnp.float32)
    offset = cell - base
    valid = (cell > 0.0) & (offset >= 0.0) & (offset < float(ext * columns))
    offset = jnp.where(valid, offset, 0.0)
    row = jnp.floor((offset + 0.5) * (1.0 / columns))
    column = (offset - row * float(columns)).astype(jnp.int32)
    row = row.astype(jnp.int32) - HALO
    row = jnp.where(row < 0, row + ext, row)
    chunk = column // LANES
    return valid, row, chunk, column - chunk * LANES


def scattered(section, key, lane, count):
    at_lane = one_hot(LANES, lane)
    parts = [at_lane] + [at_lane * part.astype(jnp.float32) for part in split3(section)]
    grid = lax.dot_general(
        one_hot(-(-count // 16) * 16, key).astype(jnp.bfloat16),
        jnp.concatenate(parts, axis=0).astype(jnp.bfloat16),
        (((1,), (1,)), ((), ())),
        preferred_element_type=jnp.float32,
    )
    number = grid[:, :LANES]
    total = (grid[:, LANES : 2 * LANES] + grid[:, 2 * LANES : 3 * LANES]) + grid[:, 3 * LANES :]
    return number, total


def pack_kernel(
    depth, bed, rough, east, south, section, cells, to_other, own, held, held_rough, held_cells, sems
):
    rows, columns = depth.shape
    even = lax.axis_index("gy") % 2 == 0
    start = pl.multiple_of(jnp.where(even, 0, rows - 8), 8)
    copies = [
        pltpu.make_async_copy(source, target, sems.at[slot])
        for slot, (source, target) in enumerate(
            (
                (depth.at[pl.ds(start, 8), :], held.at[0]),
                (bed.at[pl.ds(start, 8), :], held.at[1]),
                (rough.at[pl.ds(start, 8), :], held_rough),
                (east.at[pl.ds(start, 8), :], held.at[2]),
                (south.at[pl.ds(start, 8), :], held.at[3]),
                (section, own.at[pl.ds(0, 1), :]),
                (cells, held_cells),
            )
        )
    ]
    for copy in copies:
        copy.start()
    for slot in range(5):
        copies[slot].wait()
        block = (
            held_rough[...].astype(jnp.float32) if slot == 2 else held[slot - (slot > 2)]
        )
        to_other[slot, :, :columns] = jnp.where(even, block[:HALO], block[8 - HALO :])
        to_other[slot, :, columns:] = jnp.zeros((HALO, LANES), jnp.float32)
    for copy in copies[5:]:
        copy.wait()
    own[1:2, :] = (held_cells[0:1, :] + 1).astype(jnp.float32)
    to_other[0, 0:2, columns:] = own[...]


def join_kernel(before, section, cells, to_other):
    columns = to_other.shape[2] - LANES
    to_other[0, 2:3, columns:] = section[...]
    to_other[0, 3:4, columns:] = (cells[0:1, :] + 1).astype(jnp.float32)


def load_kernel(
    depth_in, east_in, south_in, bed_in, rough_in, to_partner, surf, east, south, bed, rough, sems
):
    rows, columns = depth_in.shape
    even = lax.axis_index("gy") % 2 == 0
    own = pl.ds(0, rows)
    copies = [
        pltpu.make_async_copy(source, target.at[own, :], sems.at[slot])
        for slot, (source, target) in enumerate(
            (
                (depth_in, surf),
                (bed_in, bed),
                (rough_in, rough),
                (east_in, east),
                (south_in, south),
            )
        )
    ]
    for copy in copies:
        copy.start()
    for slot, source in enumerate((surf, bed, rough, east, south)):
        copies[slot].wait()
        for chunk in range(columns // LANES):
            at = cols(chunk)
            first = source[:8, at].astype(jnp.float32)
            last = source[rows - 8 : rows, at].astype(jnp.float32)
            to_partner[slot, :, at] = jnp.where(even, last[8 - HALO :], first[:HALO])


def prepare_kernel(table, rough, own, partner_section, partner_cells, *refs):
    surf, east, south, bed = refs[4:8]
    mann, bed_e, bed_s, drag_e, drag_s, number, total, table_rows = refs[8:]
    ext, columns = surf.shape
    rows = ext - 2 * HALO
    chunks = columns // LANES
    tiles = lax.axis_size("gy")
    position = lax.axis_index("gy")
    side = jnp.where(position % 2 == 0, 1, -1)
    entries = [table[k] for k in range(table.shape[0])]
    for k, entry in enumerate(entries):
        table_rows[k : k + 1, :] = jnp.full((1, LANES), entry, jnp.float32)
    for chunk in range(chunks):
        at = cols(chunk)
        mann[:rows, at] = looked_up(rough[:, at], entries)
        surf[:rows, at] = surf[:rows, at] + bed[:rows, at]

    partner = jnp.where(position + side < tiles, partner_cells[0:1, :] + 1, 0).astype(jnp.float32)
    section = jnp.concatenate([own[0:1, :], partner_section[...]], axis=1)
    cell = jnp.concatenate([own[1:2, :], partner], axis=1)
    valid, node_row, node_chunk, node_lane = located(cell, position, rows, ext, columns)
    key = jnp.where(valid, node_chunk * ext + node_row, -1)
    starts, levels = scattered(section, key, node_lane, chunks * ext)
    for chunk in range(chunks):
        at = cols(chunk)
        number[:, at] = starts[chunk * ext : (chunk + 1) * ext]
        total[:, at] = levels[chunk * ext : (chunk + 1) * ext]

    kept = lax.broadcasted_iota(jnp.int32, (rows, LANES), 0) == rows - 1
    for chunk in range(chunks):
        at, then = cols(chunk), cols(min(chunk + 1, chunks - 1))
        s0, b0, m0 = surf[:rows, at], bed[:rows, at], mann[:rows, at]
        bed_max = jnp.maximum(b0, moved_left(b0, bed[:rows, then], 1))
        drag = drag_of(m0, moved_left(m0, mann[:rows, then], 1))
        bed_e[:rows, at] = bed_max
        drag_e[:rows, at] = drag
        new_east = face(
            east[:rows, at], s0, moved_left(s0, surf[:rows, then], 1), bed_max, drag
        )
        east[:rows, at] = east_walled(new_east, chunk, chunks)
        bed_max = jnp.maximum(b0, moved_up(b0))
        drag = drag_of(m0, moved_up(m0))
        bed_s[:rows, at] = bed_max
        drag_s[:rows, at] = drag
        q0 = south[:rows, at]
        south[:rows, at] = jnp.where(kept, q0, face(q0, s0, moved_up(s0), bed_max, drag))


def wall_of(ext, tiles):
    position = lax.axis_index("gy")
    rows = ext - 2 * HALO
    row = lax.broadcasted_iota(jnp.int32, (16, LANES), 0) + (ext - 16)
    return ((row == ext - 1) & (position == 0)) | ((row == rows - 1) & (position == tiles - 1))


def border_kernel(tiles, by_partner, by_other, table_rows, *refs):
    surf, east, south, bed, mann, bed_e, bed_s, drag_e, drag_s, number, total = refs[11:]
    ext, columns = surf.shape
    rows = ext - 2 * HALO
    chunks = columns // LANES
    position = lax.axis_index("gy")
    even = position % 2 == 0
    entries = [table_rows[k : k + 1, :] for k in range(table_rows.shape[0])]
    for chunk in range(chunks):
        at = cols(chunk)
        halos = []
        for slot in range(5):
            a, b = by_partner[slot, :, at], by_other[slot, :, at]
            below = jnp.where(even, a, b)
            above = jnp.where(even, b, a)
            halos.append(jnp.concatenate([below, above], axis=0))
        surf[rows:, at] = halos[0] + halos[1]
        bed[rows:, at] = halos[1]
        mann[rows:, at] = looked_up(halos[2].astype(jnp.int32), entries)
        east[rows:, at] = halos[3]
        south[rows:, at] = halos[4]

    near = by_other[0, :, columns:]
    section = jnp.concatenate([near[0:1, :], near[2:3, :]], axis=1)
    cell = jnp.concatenate([near[1:2, :], near[3:4, :]], axis=1)
    valid, node_row, node_chunk, node_lane = located(cell, position, rows, ext, columns)
    key = jnp.where(valid, node_chunk * ext + node_row, -1)
    starts, levels = scattered(section, key, node_lane, chunks * ext)

    wall = wall_of(ext, tiles)
    kept = lax.broadcasted_iota(jnp.int32, (16, LANES), 0) < 7
    for chunk in range(chunks):
        at, then = cols(chunk), cols(min(chunk + 1, chunks - 1))
        number[:, at] += starts[chunk * ext : (chunk + 1) * ext]
        total[:, at] += levels[chunk * ext : (chunk + 1) * ext]
        s0, b0, m0 = surf[rows:, at], bed[rows:, at], mann[rows:, at]
        bed_max = jnp.maximum(b0, moved_left(b0, bed[rows:, then], 1))
        drag = drag_of(m0, moved_left(m0, mann[rows:, then], 1))
        bed_e[rows:, at] = bed_max
        drag_e[rows:, at] = drag
        new_east = face(
            east[rows:, at], s0, moved_left(s0, surf[rows:, then], 1), bed_max, drag
        )
        east[rows:, at] = east_walled(new_east, chunk, chunks)

        def rolled_up(ref):
            value = jnp.concatenate([ref[rows - 8 :, at], ref[:8, at]], axis=0)
            return value[:16], moved_up(value)[:16]

        s0, s1 = rolled_up(surf)
        b0, b1 = rolled_up(bed)
        m0, m1 = rolled_up(mann)
        bed_max = jnp.maximum(b0, b1)
        drag = drag_of(m0, m1)
        bed_s[rows - 8 :, at] = bed_max
        drag_s[rows - 8 :, at] = drag
        q0 = south[rows - 8 :, at]
        new_south = jnp.where(wall, 0.0, face(q0, s0, s1, bed_max, drag))
        south[rows - 8 :, at] = jnp.where(kept, q0, new_south)


def substep(fluxes_done, last, corridor, wall, refs):
    surf, east, south, bed_e, bed_s, drag_e, drag_s, total, covers, count = refs
    ext, columns = surf.shape
    rows = ext - 2 * HALO
    chunks = columns // LANES
    tall = rows if last else ext
    lane = lanes_of(ext)
    zero = jnp.zeros((tall, LANES), jnp.float32)
    surfs, rolls, lefts, pairs, turned = {}, {}, {}, {}, {}

    def fetch(chunk):
        if chunk < chunks:
            surfs[chunk] = surf[:, cols(chunk)]
            rolls[chunk] = pltpu.roll(surfs[chunk], LANES - 1, 1)
        else:
            rolls[chunk] = rolls[chunks - 1]

    def join(chunk):
        if chunk < chunks:
            lefts[chunk] = jnp.where(lane >= LANES - 1, rolls[chunk + 1], rolls[chunk])
            if not last:
                pairs[chunk] = surfs[chunk] + lefts[chunk]
                turned[chunk] = pltpu.roll(pairs[chunk], LANES - 2, 1)
        else:
            turned[chunk] = turned.get(chunks - 1)

    fetch(0)
    fetch(1)
    join(0)
    east_last = zero
    state = (zero, zero)
    for chunk in range(chunks):
        at = cols(chunk)
        if not last:
            if chunk + 2 <= chunks:
                fetch(chunk + 2)
            join(chunk + 1)
        elif chunk > 0:
            fetch(chunk + 1)
            join(chunk)
        s0 = surfs[chunk]
        if fluxes_done:
            new_east, new_south = east[:, at], south[:, at]
        else:
            new_east = face(
                east[:tall, at], s0[:tall], lefts[chunk][:tall], bed_e[:tall, at], drag_e[:tall, at]
            )
            new_east = east_walled(new_east, chunk, chunks)
            new_south = face(south[:, at], s0, moved_up(s0), bed_s[:, at], drag_s[:, at])
            new_south = jnp.concatenate(
                [new_south[:-16], jnp.where(wall, 0.0, new_south[-16:])], axis=0
            )
        held = total[:tall, at]
        summed, state = right_sum(held, state)
        if not last:
            window = pairs[chunk] + jnp.where(
                lane >= LANES - 2, turned[chunk + 1], turned[chunk]
            )
            total[:, at] = (1.0 - corridor * DRAIN) * held + count[:, at] * window
        east_rolled = pltpu.roll(new_east, 1, 1)
        north = pltpu.roll(new_south, 1, 0)
        inflow = jnp.where(lane[:tall] < 1, east_last, east_rolled) + north[:tall]
        east_last = east_rolled
        new_surf = (
            s0[:tall]
            + SPREAD * (inflow - new_east - new_south[:tall])
            + (summed - covers[:tall, at] * s0[:tall])
        )
        yield chunk, new_surf, new_east, new_south


def steps_kernel(corridor, tiles, own, partner_cells, near, far, *refs):
    number = refs[7]
    own_term, partner_term, other_term = refs[9:12]
    surf, east, south, bed_e, bed_s, drag_e, drag_s, total, covers = refs[12:21]
    count, first_total = refs[21:]
    ext, columns = surf.shape
    rows = ext - 2 * HALO
    owned = own.shape[1]
    chunks = columns // LANES
    position = lax.axis_index("gy")
    side = jnp.where(position % 2 == 0, 1, -1)

    valid, node_row, node_chunk, node_lane = located(far[1:2, :], position, rows, ext, columns)
    key = jnp.where(valid & (node_row >= rows), node_chunk * 8 + (node_row - rows), -1)
    starts, levels = scattered(far[0:1, :], key, node_lane, chunks * 8)
    zero = jnp.zeros((ext, LANES), jnp.float32)
    state = (zero, zero)
    for chunk in range(chunks):
        at, mine = cols(chunk), slice(chunk * 8, chunk * 8 + 8)
        starting = number[:, at]
        starting = jnp.concatenate([starting[:rows], starting[rows:] + starts[mine]], axis=0)
        held = total[:, at]
        held = FEED * jnp.concatenate([held[:rows], held[rows:] + levels[mine]], axis=0)
        count[:, at] = (FEED * DRAIN) * starting
        total[:, at] = held
        first_total[:, at] = held[:rows]
        covering, state = right_sum(starting, state)
        covers[:, at] = FEED * covering

    wall = wall_of(ext, tiles)
    state_refs = (surf, east, south, bed_e, bed_s, drag_e, drag_s, total, covers, count)
    for chunk, new_surf, new_east, new_south in substep(True, False, corridor, wall, state_refs):
        surf[:, cols(chunk)] = new_surf

    def body(step, carry):
        for chunk, new_surf, new_east, new_south in substep(
            False, False, corridor, wall, state_refs
        ):
            at = cols(chunk)
            surf[:, at] = new_surf
            east[:, at] = new_east
            south[:, at] = new_south
        return carry

    lax.fori_loop(0, STEPS - 2, body, 0)

    kept = (1.0 - corridor * DRAIN) ** STEPS
    levels = []
    for chunk in range(chunks):
        at, then = cols(chunk), cols(min(chunk + 1, chunks - 1))
        window = surf[:rows, at]
        for by in range(1, corridor):
            window = window + moved_left(surf[:rows, at], surf[:rows, then], by)
        starting = count[:rows, at]
        held = (1.0 - corridor * DRAIN) * total[:rows, at] + starting * window
        gained = held - kept * first_total[:, at]
        weight = jnp.maximum(starting * (1.0 / DRAIN), FEED)
        levels.append(gained * pl.reciprocal(weight, approx=True))
    partner = jnp.where(position + side < tiles, partner_cells[0:1, :] + 1, 0).astype(jnp.float32)
    cell = jnp.concatenate([own[1:2, :], partner, near[1:2, :]], axis=1)
    valid, node_row, node_chunk, node_lane = located(cell, position, rows, ext, columns)
    take_key = jnp.where(valid & (node_row < rows), node_chunk * rows + node_row, -1)
    takes = one_hot(chunks * rows, take_key).astype(jnp.bfloat16)
    picked = lax.dot_general(
        jnp.concatenate(split3(jnp.concatenate(levels, axis=0)), axis=1),
        takes,
        (((0,), (0,)), ((), ())),
        preferred_element_type=jnp.float32,
    )
    picked = (picked[:LANES] + picked[LANES : 2 * LANES]) + picked[2 * LANES :]
    terms = jnp.sum(picked * one_hot(LANES, node_lane), axis=0, keepdims=True)
    own_term[...] = kept * own[0:1, :] + terms[:, :owned]
    partner_term[...] = terms[:, owned : 2 * owned]
    other_term[...] = terms[:, 2 * owned :]


def last_kernel(corridor, tiles, *refs):
    bed = refs[9]
    targets = refs[10:13]
    results = refs[13:16]
    sems = refs[16]
    ext, columns = bed.shape
    rows = ext - 2 * HALO
    chunks = columns // LANES
    group = 5
    copies = []
    steps = substep(False, True, corridor, wall_of(ext, tiles), refs[:9] + (None,))
    for chunk, new_surf, new_east, new_south in steps:
        at = cols(chunk)
        results[0][:, at] = new_surf - bed[:rows, at]
        results[1][:, at] = new_east
        results[2][:, at] = new_south[:rows]
        if (chunk + 1) % group == 0 or chunk + 1 == chunks:
            first = chunk // group * group * LANES
            width = pl.ds(first, (chunk + 1) * LANES - first)
            for slot, (result, target) in enumerate(zip(results, targets)):
                copy = pltpu.make_async_copy(
                    result.at[:, width], target.at[:, width], sems.at[chunk // group, slot]
                )
                copy.start()
                copies.append(copy)
    for copy in copies:
        copy.wait()


def local(
    depth, flux_east, flux_south, river_section, bed_level, rough_class, manning_table, bank_cell
):
    rows, columns = depth.shape
    owned = river_section.shape[0]
    corridor = bank_cell.shape[0]
    tiles = lax.axis_size("gy")
    ext = rows + 2 * HALO
    chunks = columns // LANES
    partner_section = swapped(river_section, 0).reshape(1, owned)
    partner_cells = swapped(bank_cell, 0)

    def held(value):
        return pltpu.with_memory_space_constraint(value, pltpu.VMEM)

    def far(value):
        return pltpu.with_memory_space_constraint(value, pltpu.HBM)

    params = pltpu.CompilerParams(vmem_limit_bytes=VMEM_LIMIT)
    halo = pltpu.VMEM((5, HALO, columns), jnp.float32)
    field = pltpu.VMEM((ext, columns), jnp.float32)
    term = pltpu.VMEM((1, owned), jnp.float32)
    wide = pltpu.VMEM((5, HALO, columns + LANES), jnp.float32)
    to_other, own = pl.pallas_call(
        pack_kernel,
        out_shape=[wide, pltpu.VMEM((2, owned), jnp.float32)],
        in_specs=[HBM_SPEC] * 7,
        out_specs=[VMEM_SPEC] * 2,
        scratch_shapes=[
            pltpu.VMEM((4, 8, columns), jnp.float32),
            pltpu.VMEM((8, columns), jnp.int32),
            pltpu.VMEM((corridor, owned), jnp.int32),
            pltpu.SemaphoreType.DMA((7,)),
        ],
        compiler_params=params,
        name="pack",
    )(
        *[far(value) for value in (depth, bed_level, rough_class, flux_east, flux_south)],
        far(river_section.reshape(1, owned)),
        far(bank_cell),
    )
    to_other = pl.pallas_call(
        join_kernel,
        out_shape=wide,
        in_specs=[VMEM_SPEC] * 3,
        out_specs=VMEM_SPEC,
        input_output_aliases={0: 0},
        compiler_params=params,
        name="join",
    )(held(to_other), held(partner_section), held(partner_cells))
    by_other = swapped(to_other, 1)
    from_far = swapped(by_other[0, 0:2, columns:], 0)
    to_partner, *loaded, rough = pl.pallas_call(
        load_kernel,
        out_shape=[halo] + [field] * 4 + [pltpu.VMEM((rows, columns), jnp.int32)],
        in_specs=[HBM_SPEC] * 5,
        out_specs=[VMEM_SPEC] * 6,
        scratch_shapes=[pltpu.SemaphoreType.DMA((5,))],
        compiler_params=params,
        name="load",
    )(*[far(value) for value in (depth, flux_east, flux_south, bed_level, rough_class)])
    by_partner = swapped(to_partner, 0)
    *fields, table_rows = pl.pallas_call(
        prepare_kernel,
        out_shape=[field] * 11 + [pltpu.VMEM((manning_table.shape[0], LANES), jnp.float32)],
        in_specs=[SMEM_SPEC] + [VMEM_SPEC] * 8,
        out_specs=[VMEM_SPEC] * 12,
        input_output_aliases={5 + slot: slot for slot in range(4)},
        compiler_params=params,
        name="prepare",
    )(
        manning_table,
        *[held(value) for value in (rough, own, partner_section, partner_cells, *loaded)],
    )
    near = by_other[0, 0:2, columns:]
    from_far = swapped(near, 0)
    fields = pl.pallas_call(
        functools.partial(border_kernel, tiles),
        out_shape=[field] * 11,
        in_specs=[VMEM_SPEC] * 14,
        out_specs=[VMEM_SPEC] * 11,
        input_output_aliases={3 + slot: slot for slot in range(11)},
        compiler_params=params,
        name="border",
    )(*[held(value) for value in (by_partner, by_other, table_rows, *fields)])
    surf, east, south, bed, _, bed_e, bed_s, drag_e, drag_s, number, total = fields
    stepped = pl.pallas_call(
        functools.partial(steps_kernel, corridor, tiles),
        out_shape=[term] * 3 + [field] * 9,
        in_specs=[VMEM_SPEC] * 13,
        out_specs=[VMEM_SPEC] * 12,
        scratch_shapes=[field, pltpu.VMEM((rows, columns), jnp.float32)],
        input_output_aliases={4 + slot: 3 + slot for slot in range(7)} | {12: 10},
        compiler_params=params,
        name="steps",
    )(
        *[held(value) for value in (own, partner_cells, near, from_far)],
        *[held(value) for value in (surf, east, south, bed_e, bed_s, drag_e, drag_s)],
        *[held(value) for value in (number, total)],
    )
    from_other = swapped(stepped[2].reshape(owned), 1)
    from_partner = swapped(stepped[1].reshape(owned), 0)
    result = pltpu.HBM((rows, columns), jnp.float32)
    depth, flux_east, flux_south = pl.pallas_call(
        functools.partial(last_kernel, corridor, tiles),
        out_shape=[result] * 3,
        in_specs=[VMEM_SPEC] * 10,
        out_specs=[HBM_SPEC] * 3,
        scratch_shapes=[pltpu.VMEM((rows, columns), jnp.float32)] * 3
        + [pltpu.SemaphoreType.DMA((-(-chunks // 5), 3))],
        compiler_params=params,
        name="last",
    )(*[held(value) for value in (*stepped[3:], bed)])
    river_section = stepped[0].reshape(owned) + from_partner + from_other
    return (depth, flux_east, flux_south, river_section)


def solution(mesh):
    return jax.shard_map(
        local,
        mesh=mesh,
        in_specs=(
            P(("runs", "gy"), None),
            P(("runs", "gy"), None),
            P(("runs", "gy"), None),
            P(("runs", "gy")),
            P("gy", None),
            P("gy", None),
            P(),
            P(None, "gy"),
        ),
        out_specs=(
            P(("runs", "gy"), None),
            P(("runs", "gy"), None),
            P(("runs", "gy"), None),
            P(("runs", "gy")),
        ),
        check_vma=False,
    )
```

profile of v0, /device:TPU:7, one launch (start us, length us, event | category | flops | bytes accessed | tf_op | source)
XLA Modules:
  0.0 26.9 jit_solution(17614453549423136991)
XLA Ops:
  0.6 0.7 %collective-permute-start = (s32[4,128]{1,0:T(4,128)}, s32[4,128]{1,0:T(4,128)S(1)}, u32[]{:S(2)}, u32[]{:S(2)}) collective-permute-start(s32[4,128]{1,0:T(4,128)} %cells.1), channel_id=1, source_target_pairs={{0,1},{1,0},{2,3},{3,2},{4,5},{5,4},{6,7},{7,6},{8,9},{9,8},{10,11... | collective-permute-start | bytes 6152 | tf_op jit(solution)/shard_map/ppermute | solution.py:38
  1.4 0.1 collective-permute-start.1
  1.4 1.0 %pack.1 = (f32[5,4,2048]{2,1,0:T(4,128)S(1)}, f32[2,128]{1,0:T(2,128)S(1)}) custom-call(f32[32,1920]{1,0:T(8,128)} %depth_in.1, f32[32,1920]{1,0:T(8,128)} %bed_in.1, s32[32,1920]{1,0:T(8,128)} %rough_in.1, f32[32,1920]{1,0:T(8,128)} %east_in.1, f32[32,1920]{1,0:T(8,128)} %south_in.1, f32[1,128]{1,0:T(1,128)} %bitcast.14, s32[4,128]{1,0:T(4,128)} %cells.1), custom_call_target="tpu_custom_call" | custom-call | tf_op jit(solution)/shard_map/pack/pallas_call | solution.py:520
  2.5 0.1 collective-permute-done.1
  2.6 0.0 collective-permute-done.cells.partner_cells
  2.6 3.3 %collective-permute-start.2 = (f32[5,4,2048]{2,1,0:T(4,128)S(1)}, f32[5,4,2048]{2,1,0:T(4,128)S(1)}, u32[]{:S(2)}, u32[]{:S(2)}) collective-permute-start(f32[5,4,2048]{2,1,0:T(4,128)S(1)} %join.1), channel_id=1, source_target_pairs={{1,2},{2,1},{3,4},{4,3},{5,6},{6,5},{7,8},{8,7},{9,10},{10,9},{11,... | collective-permute-start | bytes 491528 | tf_op jit(solution)/shard_map/ppermute | solution.py:38
  6.0 1.4 %load.1 = (f32[5,4,1920]{2,1,0:T(4,128)S(1)}, f32[40,1920]{1,0:T(8,128)S(1)}, f32[40,1920]{1,0:T(8,128)S(1)}, f32[40,1920]{1,0:T(8,128)S(1)}, f32[40,1920]{1,0:T(8,128)S(1)}, /*index=5*/s32[32,1920]{1,0:T(8,128)S(1)}) custom-call(f32[32,1920]{1,0:T(8,128)} %depth_in.1, f32[32,1920]{1,0:T(8,128)} %east_in.1, f32[32,1920]{1,0:T(8,128)} %south_in.1, ...), custom_call_target="tpu_custom_call" | custom-call | tf_op jit(solution)/shard_map/load/pallas_call | solution.py:549
  7.4 0.1 collective-permute-start.4
  7.5 2.8 %collective-permute-done.2.by_other = f32[5,4,2048]{2,1,0:T(4,128)S(1)} collective-permute-done((f32[5,4,2048]{2,1,0:T(4,128)S(1)}, f32[5,4,2048]{2,1,0:T(4,128)S(1)}, u32[]{:S(2)}, u32[]{:S(2)}) %collective-permute-start.2) | collective-permute-done | bytes 163872 | tf_op jit(solution)/shard_map/ppermute | solution.py:38
  10.3 1.1 %collective-permute-start.3 = (f32[2,128]{1,0:T(2,128)S(1)}, f32[2,128]{1,0:T(2,128)S(1)}, u32[]{:S(2)}, u32[]{:S(2)}) collective-permute-start(f32[2,128]{1,0:T(2,128)S(1)} %slice_bitcast_fusion.near), channel_id=1, source_target_pairs={{0,1},{1,0},{2,3},{3,2},{4,5},{5,4},{6,7},{7,6},{8,9},{9,8},{10,11... | collective-permute-start | bytes 3080 | tf_op jit(solution)/shard_map/ppermute | solution.py:38
  11.3 0.0 copy-start
  11.3 0.7 %copy-done = f32[8]{0:T(128)S(1)} copy-done((f32[8]{0:T(128)S(1)}, f32[8]{0:T(128)}, u32[]{:S(2)}) %copy-start) | copy-done | bytes 56
  12.0 1.3 %prepare.1 = (f32[40,1920]{1,0:T(8,128)S(1)}, f32[40,1920]{1,0:T(8,128)S(1)}, f32[40,1920]{1,0:T(8,128)S(1)}, f32[40,1920]{1,0:T(8,128)S(1)}, f32[40,1920]{1,0:T...) custom-call(f32[8]{0:T(128)S(1)} %copy-done, ...), custom_call_target="tpu_custom_call", output_to_operand_aliasing={{0}: (5, {}), {1}: (6, {}), {2}: (7, {}), {3}: (8, {})} | custom-call | tf_op jit(solution)/shard_map/prepare/pallas_call | solution.py:559
  13.3 0.0 collective-permute-done.4.by_partner
  13.3 0.5 %border.1 = (f32[40,1920]{1,0:T(8,128)S(1)}, f32[40,1920]{1,0:T(8,128)S(1)}, f32[40,1920]{1,0:T(8,128)S(1)}, f32[40,1920]{1,0:T(8,128)S(1)}, f32[40,1920]{1,0:T(...) custom-call(f32[5,4,1920]{2,1,0:T(4,128)S(1)} %collective-permute-do, ...), custom_call_target="tpu_custom_call", output_to_operand_aliasing={{0}: (3, {}), {1}: (4, {}), {2}: (5, {}), {3}: (6, {}), {4}... | custom-call | tf_op jit(solution)/shard_map/border/pallas_call | solution.py:573
  13.8 0.0 collective-permute-done.3.far
  13.8 6.7 %steps.1 = (f32[1,128]{1,0:T(1,128)S(1)}, f32[1,128]{1,0:T(1,128)S(1)}, f32[1,128]{1,0:T(1,128)S(1)}, f32[40,1920]{1,0:T(8,128)S(1)}, f32[40,1920]{1,0:T(8,128)S...) custom-call(f32[2,128]{1,0:T(2,128)S(1)} %get-tuple-element.49.own, ...), custom_call_target="tpu_custom_call", output_to_operand_aliasing={{3}: (4, {}), {4}: (5, {}), {5}: (6, {}), {6}: (7, {}), {7}... | custom-call | tf_op jit(solution)/shard_map/steps/pallas_call | solution.py:583
  20.6 0.1 collective-permute-start.5
  20.6 3.2 %collective-permute-start.6 = (f32[128]{0:T(128)S(1)}, f32[128]{0:T(128)S(1)}, u32[]{:S(2)}, u32[]{:S(2)}) collective-permute-start(f32[128]{0:T(128)S(1)} %bitcast.12), channel_id=1, source_target_pairs={{1,2},{2,1},{3,4},{4,3},{5,6},{6,5},{7,8},{8,7},{9,10},{10,9},{11,... | collective-permute-start | bytes 1544 | tf_op jit(solution)/shard_map/ppermute | solution.py:38
  23.9 1.6 %last.1 = (f32[32,1920]{1,0:T(8,128)}, f32[32,1920]{1,0:T(8,128)}, f32[32,1920]{1,0:T(8,128)}) custom-call(f32[40,1920]{1,0:T(8,128)S(1)} %get-tuple-element.78.refs_0_, f32[40,1920]{1,0:T(8,128)S(1)} %get-tuple-element.79.refs_1_, f32[40,1920]{1,0:T(8,128)S(1)} %get-tuple-element.80.refs_2_, f32[40,1920]{1,0:T(8,128)S(1)} %get-tuple-element.81.refs_3_, ...), custom_call_target="tpu_custom_call" | custom-call | tf_op jit(solution)/shard_map/last/pallas_call | solution.py:600
  25.4 0.0 collective-permute-done.5
  25.5 0.9 %collective-permute-done.6 = f32[128]{0:T(128)S(1)} collective-permute-done((f32[128]{0:T(128)S(1)}, f32[128]{0:T(128)S(1)}, u32[]{:S(2)}, u32[]{:S(2)}) %collective-permute-start.6) | collective-permute-done | bytes 544 | tf_op jit(solution)/shard_map/ppermute | solution.py:38
  26.4 0.5 %fusion = f32[128]{0:T(128)} fusion(f32[128]{0:T(128)S(1)} %collective-permute-done.6, f32[128]{0:T(128)S(1)} %collective-permute-done.5, f32[1,128]{1,0:T(1,128)S(1)} %get-tuple-element.91), kind=kLoop, calls=%fused_computation.2 | loop fusion | flops 256 | bytes 2048 | tf_op jit(solution)/shard_map/add | solution.py:610
  (2 shorter events, 0.0 us)
Async XLA Ops:
  0.6 2.0 %collective-permute-start = (s32[4,128]{1,0:T(4,128)}, s32[4,128]{1,0:T(4,128)S(1)}, u32[]{:S(2)}, u32[]{:S(2)}) collective-permute-start(s32[4,128]{1,0:T(4,128)} %cells.1), channel_id=1, source_target_pairs={{0,1},{1,0},{2,3},{3,2},{4,5},{5,4},{6,7},{7,6},{8,9},{9,8},{10,11... | collective-permute-start | bytes 6152 | tf_op jit(solution)/shard_map/ppermute | solution.py:38
  1.4 1.3 %collective-permute-start.1 = (f32[128]{0:T(128)}, f32[128]{0:T(128)S(1)}, u32[]{:S(2)}, u32[]{:S(2)}) collective-permute-start(f32[128]{0:T(128)} %param.11), channel_id=1, source_target_pairs={{0,1},{1,0},{2,3},{3,2},{4,5},{5,4},{6,7},{7,6},{8,9},{9,8},{10,11... | collective-permute-start | bytes 1544 | tf_op jit(solution)/shard_map/ppermute | solution.py:38
  2.6 7.6 %collective-permute-start.2 = (f32[5,4,2048]{2,1,0:T(4,128)S(1)}, f32[5,4,2048]{2,1,0:T(4,128)S(1)}, u32[]{:S(2)}, u32[]{:S(2)}) collective-permute-start(f32[5,4,2048]{2,1,0:T(4,128)S(1)} %join.1), channel_id=1, source_target_pairs={{1,2},{2,1},{3,4},{4,3},{5,6},{6,5},{7,8},{8,7},{9,10},{10,9},{11,... | collective-permute-start | bytes 491528 | tf_op jit(solution)/shard_map/ppermute | solution.py:38
  7.4 5.8 %collective-permute-start.4 = (f32[5,4,1920]{2,1,0:T(4,128)S(1)}, f32[5,4,1920]{2,1,0:T(4,128)S(1)}, u32[]{:S(2)}, u32[]{:S(2)}) collective-permute-start(f32[5,4,1920]{2,1,0:T(4,128)S(1)} %get-tuple-element.51), channel_id=1, source_target_pairs={{0,1},{1,0},{2,3},{3,2},{4,5},{5,4},{6,7},{7,6},{8,9},{9,8},{10,11... | collective-permute-start | bytes 460808 | tf_op jit(solution)/shard_map/ppermute | solution.py:38
  10.3 3.6 %collective-permute-start.3 = (f32[2,128]{1,0:T(2,128)S(1)}, f32[2,128]{1,0:T(2,128)S(1)}, u32[]{:S(2)}, u32[]{:S(2)}) collective-permute-start(f32[2,128]{1,0:T(2,128)S(1)} %slice_bitcast_fusion.near), channel_id=1, source_target_pairs={{0,1},{1,0},{2,3},{3,2},{4,5},{5,4},{6,7},{7,6},{8,9},{9,8},{10,11... | collective-permute-start | bytes 3080 | tf_op jit(solution)/shard_map/ppermute | solution.py:38
  11.3 0.7 %copy-start = (f32[8]{0:T(128)S(1)}, f32[8]{0:T(128)}, u32[]{:S(2)}) copy-start(f32[8]{0:T(128)} %table.1) | copy-start | bytes 100
  20.6 4.9 %collective-permute-start.5 = (f32[128]{0:T(128)S(1)}, f32[128]{0:T(128)S(1)}, u32[]{:S(2)}, u32[]{:S(2)}) collective-permute-start(f32[128]{0:T(128)S(1)} %bitcast.13), channel_id=1, source_target_pairs={{0,1},{1,0},{2,3},{3,2},{4,5},{5,4},{6,7},{7,6},{8,9},{9,8},{10,11... | collective-permute-start | bytes 1544 | tf_op jit(solution)/shard_map/ppermute | solution.py:38
  20.6 5.8 %collective-permute-start.6 = (f32[128]{0:T(128)S(1)}, f32[128]{0:T(128)S(1)}, u32[]{:S(2)}, u32[]{:S(2)}) collective-permute-start(f32[128]{0:T(128)S(1)} %bitcast.12), channel_id=1, source_target_pairs={{1,2},{2,1},{3,4},{4,3},{5,6},{6,5},{7,8},{8,7},{9,10},{10,9},{11,... | collective-permute-start | bytes 1544 | tf_op jit(solution)/shard_map/ppermute | solution.py:38
where the time goes:
time: 27.3 us; the launch traced here: 26.9 us
  Pallas kernels  12.6 us (46%)
  starting transfers between devices  8.59 us (31%)
  waiting for transfers between devices  3.84 us (14%)
  between operations  0.74 us (3%)
  local copies, waits for them, and re-layouts  0.66 us (2%)
  other arithmetic  0.51 us (2%)
    ppermute x7, starting transfers between devices, swapped(): return lax.ppermute(value, 'gy', pairs)  8.59 us
    pallas_call x1, Pallas kernels, local(): pl.pallas_call(functools.partial(steps_kernel, corridor, tiles), out_shap...  6.7 us
    ppermute x7, waiting for transfers between devices, swapped(): return lax.ppermute(value, 'gy', pairs)  3.84 us
    pallas_call x1, Pallas kernels, local(): pl.pallas_call(functools.partial(last_kernel, corridor, tiles), out_shape...  1.58 us
    pallas_call x1, Pallas kernels, local(): pl.pallas_call(load_kernel, out_shape=[halo] + [field] * 4 + [pltpu.VMEM(...  1.44 us
    pallas_call x1, Pallas kernels, local(): pl.pallas_call(prepare_kernel, out_shape=[field] * 11 + [pltpu.VMEM((mann...  1.27 us
    pallas_call x1, Pallas kernels, local(): pl.pallas_call(pack_kernel, out_shape=[wide, pltpu.VMEM((2, owned), jnp.f...  1.02 us
    unnamed x2, local copies, waits for them, and re-layouts  0.65 us
  transfers between devices with their start and end apart: 7, of which 3 were waited for; matrix products, arithmetic and copies ran while one was open for 0% of the time, Pallas kernels for 22%

commit v1 on v0

--- a/solution.py
+++ b/solution.py
@@ -202,6 +202,12 @@
             to_partner[slot, :, at] = jnp.where(even, last[8 - HALO :], first[:HALO])
 
 
+def relay_kernel(by_other, prepared, near):
+    del prepared
+    columns = by_other.shape[2] - LANES
+    near[...] = by_other[0, 0:2, columns:]
+
+
 def prepare_kernel(table, rough, own, partner_section, partner_cells, *refs):
     surf, east, south, bed = refs[4:8]
     mann, bed_e, bed_s, drag_e, drag_s, number, total, table_rows = refs[8:]
@@ -318,82 +324,82 @@
         south[rows - 8 :, at] = jnp.where(kept, q0, new_south)
 
 
-def substep(fluxes_done, last, corridor, wall, refs):
-    surf, east, south, bed_e, bed_s, drag_e, drag_s, total, covers, count = refs
+def exchange(corridor, surf, total, covers, count, gain):
+    ext, columns = surf.shape
+    chunks = columns // LANES
+    lane = lanes_of(ext)
+    zero = jnp.zeros((ext, LANES), jnp.float32)
+    state = (zero, zero)
+
+    def paired(value, rolled, rolled_then):
+        pair = value + jnp.where(lane >= LANES - 1, rolled_then, rolled)
+        return pair, pltpu.roll(pair, LANES - 2, 1)
+
+    values = [surf[:, cols(0)], surf[:, cols(1)]]
+    rolls = [pltpu.roll(value, LANES - 1, 1) for value in values]
+    pair, turned = paired(values[0], rolls[0], rolls[1])
+    for chunk in range(chunks):
+        at = cols(chunk)
+        if chunk + 1 < chunks:
+            if chunk + 2 < chunks:
+                ahead = surf[:, cols(chunk + 2)]
+                rolled_ahead = pltpu.roll(ahead, LANES - 1, 1)
+            else:
+                ahead, rolled_ahead = values[1], rolls[1]
+            pair_then, turned_then = paired(values[1], rolls[1], rolled_ahead)
+        else:
+            pair_then, turned_then = pair, turned
+        window = pair + jnp.where(lane >= LANES - 2, turned_then, turned)
+        held = total[:, at]
+        summed, state = right_sum(held, state)
+        gain[:, at] = summed - covers[:, at] * values[0]
+        total[:, at] = (1.0 - corridor * DRAIN) * held + count[:, at] * window
+        values, rolls = [values[1], ahead], [rolls[1], rolled_ahead]
+        pair, turned = pair_then, turned_then
+
+
+def substep(fluxes_done, last, wall, gained, refs):
+    surf, east, south, bed_e, bed_s, drag_e, drag_s = refs
     ext, columns = surf.shape
     rows = ext - 2 * HALO
     chunks = columns // LANES
     tall = rows if last else ext
-    lane = lanes_of(ext)
-    zero = jnp.zeros((tall, LANES), jnp.float32)
-    surfs, rolls, lefts, pairs, turned = {}, {}, {}, {}, {}
-
-    def fetch(chunk):
-        if chunk < chunks:
-            surfs[chunk] = surf[:, cols(chunk)]
-            rolls[chunk] = pltpu.roll(surfs[chunk], LANES - 1, 1)
+    lane = lanes_of(tall)
+    s0 = surf[:, cols(0)]
+    rolled = pltpu.roll(s0[:tall], LANES - 1, 1)
+    east_last = jnp.zeros((tall, LANES), jnp.float32)
+    for chunk in range(chunks):
+        at = cols(chunk)
+        if chunk + 1 < chunks:
+            s1 = surf[:, cols(chunk + 1)]
+            rolled_then = pltpu.roll(s1[:tall], LANES - 1, 1)
         else:
-            rolls[chunk] = rolls[chunks - 1]
-
-    def join(chunk):
-        if chunk < chunks:
-            lefts[chunk] = jnp.where(lane >= LANES - 1, rolls[chunk + 1], rolls[chunk])
-            if not last:
-                pairs[chunk] = surfs[chunk] + lefts[chunk]
-                turned[chunk] = pltpu.roll(pairs[chunk], LANES - 2, 1)
-        else:
-            turned[chunk] = turned.get(chunks - 1)
-
-    fetch(0)
-    fetch(1)
-    join(0)
-    east_last = zero
-    state = (zero, zero)
-    for chunk in range(chunks):
-        at = cols(chunk)
-        if not last:
-            if chunk + 2 <= chunks:
-                fetch(chunk + 2)
-            join(chunk + 1)
-        elif chunk > 0:
-            fetch(chunk + 1)
-            join(chunk)
-        s0 = surfs[chunk]
+            s1, rolled_then = s0, rolled
         if fluxes_done:
             new_east, new_south = east[:, at], south[:, at]
         else:
-            new_east = face(
-                east[:tall, at], s0[:tall], lefts[chunk][:tall], bed_e[:tall, at], drag_e[:tall, at]
-            )
+            left = jnp.where(lane >= LANES - 1, rolled_then, rolled)
+            new_east = face(east[:tall, at], s0[:tall], left, bed_e[:tall, at], drag_e[:tall, at])
             new_east = east_walled(new_east, chunk, chunks)
             new_south = face(south[:, at], s0, moved_up(s0), bed_s[:, at], drag_s[:, at])
             new_south = jnp.concatenate(
                 [new_south[:-16], jnp.where(wall, 0.0, new_south[-16:])], axis=0
             )
-        held = total[:tall, at]
-        summed, state = right_sum(held, state)
-        if not last:
-            window = pairs[chunk] + jnp.where(
-                lane >= LANES - 2, turned[chunk + 1], turned[chunk]
-            )
-            total[:, at] = (1.0 - corridor * DRAIN) * held + count[:, at] * window
         east_rolled = pltpu.roll(new_east, 1, 1)
         north = pltpu.roll(new_south, 1, 0)
-        inflow = jnp.where(lane[:tall] < 1, east_last, east_rolled) + north[:tall]
+        inflow = jnp.where(lane < 1, east_last, east_rolled) + north[:tall]
         east_last = east_rolled
-        new_surf = (
-            s0[:tall]
-            + SPREAD * (inflow - new_east - new_south[:tall])
-            + (summed - covers[:tall, at] * s0[:tall])
-        )
+        outflow = new_east + new_south[:tall]
+        new_surf = s0[:tall] + SPREAD * (inflow - outflow) + gained(chunk, s0)
         yield chunk, new_surf, new_east, new_south
+        s0, rolled = s1, rolled_then
 
 
 def steps_kernel(corridor, tiles, own, partner_cells, near, far, *refs):
     number = refs[7]
     own_term, partner_term, other_term = refs[9:12]
     surf, east, south, bed_e, bed_s, drag_e, drag_s, total, covers = refs[12:21]
-    count, first_total = refs[21:]
+    count, first_total, gain = refs[21:]
     ext, columns = surf.shape
     rows = ext - 2 * HALO
     owned = own.shape[1]
@@ -419,13 +425,19 @@
         covers[:, at] = FEED * covering
 
     wall = wall_of(ext, tiles)
-    state_refs = (surf, east, south, bed_e, bed_s, drag_e, drag_s, total, covers, count)
-    for chunk, new_surf, new_east, new_south in substep(True, False, corridor, wall, state_refs):
+    state_refs = (surf, east, south, bed_e, bed_s, drag_e, drag_s)
+
+    def gained(chunk, value):
+        return gain[:, cols(chunk)]
+
+    exchange(corridor, surf, total, covers, count, gain)
+    for chunk, new_surf, _, _ in substep(True, False, wall, gained, state_refs):
         surf[:, cols(chunk)] = new_surf
 
     def body(step, carry):
+        exchange(corridor, surf, total, covers, count, gain)
         for chunk, new_surf, new_east, new_south in substep(
-            False, False, corridor, wall, state_refs
+            False, False, wall, gained, state_refs
         ):
             at = cols(chunk)
             surf[:, at] = new_surf
@@ -465,8 +477,8 @@
     other_term[...] = terms[:, 2 * owned :]
 
 
-def last_kernel(corridor, tiles, *refs):
-    bed = refs[9]
+def last_kernel(tiles, *refs):
+    total, covers, bed = refs[7:10]
     targets = refs[10:13]
     results = refs[13:16]
     sems = refs[16]
@@ -475,7 +487,15 @@
     chunks = columns // LANES
     group = 5
     copies = []
-    steps = substep(False, True, corridor, wall_of(ext, tiles), refs[:9] + (None,))
+    zero = jnp.zeros((rows, LANES), jnp.float32)
+    state = [(zero, zero)]
+
+    def gained(chunk, value):
+        at = cols(chunk)
+        summed, state[0] = right_sum(total[:rows, at], state[0])
+        return summed - covers[:rows, at] * value[:rows]
+
+    steps = substep(False, True, wall_of(ext, tiles), gained, refs[:7])
     for chunk, new_surf, new_east, new_south in steps:
         at = cols(chunk)
         results[0][:, at] = new_surf - bed[:rows, at]
@@ -568,7 +588,14 @@
         manning_table,
         *[held(value) for value in (rough, own, partner_section, partner_cells, *loaded)],
     )
-    near = by_other[0, 0:2, columns:]
+    near = pl.pallas_call(
+        relay_kernel,
+        out_shape=pltpu.VMEM((2, owned), jnp.float32),
+        in_specs=[VMEM_SPEC] * 2,
+        out_specs=VMEM_SPEC,
+        compiler_params=params,
+        name="relay",
+    )(held(by_other), held(table_rows))
     from_far = swapped(near, 0)
     fields = pl.pallas_call(
         functools.partial(border_kernel, tiles),
@@ -585,7 +612,7 @@
         out_shape=[term] * 3 + [field] * 9,
         in_specs=[VMEM_SPEC] * 13,
         out_specs=[VMEM_SPEC] * 12,
-        scratch_shapes=[field, pltpu.VMEM((rows, columns), jnp.float32)],
+        scratch_shapes=[field, pltpu.VMEM((rows, columns), jnp.float32), field],
         input_output_aliases={4 + slot: 3 + slot for slot in range(7)} | {12: 10},
         compiler_params=params,
         name="steps",
@@ -598,7 +625,7 @@
     from_partner = swapped(stepped[1].reshape(owned), 0)
     result = pltpu.HBM((rows, columns), jnp.float32)
     depth, flux_east, flux_south = pl.pallas_call(
-        functools.partial(last_kernel, corridor, tiles),
+        functools.partial(last_kernel, tiles),
         out_shape=[result] * 3,
         in_specs=[VMEM_SPEC] * 10,
         out_specs=[HBM_SPEC] * 3,

time: 27.3 us -> 28.2 us (1.033)
  Pallas kernels: 12.6 us -> 15.1 us
  waiting for transfers between devices: 3.84 us -> 2 us
  starting transfers between devices: 8.59 us -> 8.9 us
    pallas_call x1, Pallas kernels: 6.7 us -> 9.07 us  [local(): pl.pallas_call(functools.partial(steps_kernel, corridor, tiles), out_shap...]
    ppermute x7, waiting for transfers between devices: 3.84 us -> 2 us  [swapped(): return lax.ppermute(value, 'gy', pairs)]
    ppermute x7, starting transfers between devices: 8.59 us -> 8.9 us  [swapped(): return lax.ppermute(value, 'gy', pairs)]
    pallas_call x1 -> x2, Pallas kernels: 1.58 us -> 1.78 us  [the longest x1 1.78 us: local(): pl.pallas_call(functools.partial(last_kernel, tiles), out_shape=[result]...]
  transfers between devices with their start and end apart: 7 -> 7, of which waited for: 3 -> 4; matrix products, arithmetic and copies ran while one was open for 0% -> 0% of each run, Pallas kernels for 22% -> 22%
where the time goes in v1:
time: 28.2 us; the launch traced here: 27.9 us
  Pallas kernels  15.1 us (54%)
  starting transfers between devices  8.9 us (32%)
  waiting for transfers between devices  2 us (7%)
  between operations  0.72 us (3%)
  local copies, waits for them, and re-layouts  0.65 us (2%)
  other arithmetic  0.51 us (2%)
    pallas_call x1, Pallas kernels, local(): pl.pallas_call(functools.partial(steps_kernel, corridor, tiles), out_shap...  9.07 us
    ppermute x7, starting transfers between devices, swapped(): return lax.ppermute(value, 'gy', pairs)  8.9 us
    ppermute x7, waiting for transfers between devices, swapped(): return lax.ppermute(value, 'gy', pairs)  2 us
    pallas_call x1, Pallas kernels, local(): pl.pallas_call(functools.partial(last_kernel, tiles), out_shape=[result]...  1.78 us
    pallas_call x1, Pallas kernels, local(): pl.pallas_call(load_kernel, out_shape=[halo] + [field] * 4 + [pltpu.VMEM(...  1.44 us
    pallas_call x1, Pallas kernels, local(): pl.pallas_call(prepare_kernel, out_shape=[field] * 11 + [pltpu.VMEM((mann...  1.27 us
    pallas_call x1, Pallas kernels, local(): pl.pallas_call(pack_kernel, out_shape=[wide, pltpu.VMEM((2, owned), jnp.f...  1.02 us
    unnamed x2, local copies, waits for them, and re-layouts  0.65 us
  transfers between devices with their start and end apart: 7, of which 4 were waited for; matrix products, arithmetic and copies ran while one was open for 0% of the time, Pallas kernels for 22%

profile of v1, /device:TPU:7, one launch (start us, length us, event | category | flops | bytes accessed | tf_op | source)
XLA Modules:
  0.0 27.9 jit_solution(6267775447737905681)
XLA Ops:
  0.6 0.7 %collective-permute-start = (s32[4,128]{1,0:T(4,128)}, s32[4,128]{1,0:T(4,128)S(1)}, u32[]{:S(2)}, u32[]{:S(2)}) collective-permute-start(s32[4,128]{1,0:T(4,128)} %cells.1), channel_id=1, source_target_pairs={{0,1},{1,0},{2,3},{3,2},{4,5},{5,4},{6,7},{7,6},{8,9},{9,8},{10,11... | collective-permute-start | bytes 6152 | tf_op jit(solution)/shard_map/ppermute | solution.py:38
  1.4 0.1 collective-permute-start.1
  1.4 1.0 %pack.1 = (f32[5,4,2048]{2,1,0:T(4,128)S(1)}, f32[2,128]{1,0:T(2,128)S(1)}) custom-call(f32[32,1920]{1,0:T(8,128)} %depth_in.1, f32[32,1920]{1,0:T(8,128)} %bed_in.1, s32[32,1920]{1,0:T(8,128)} %rough_in.1, f32[32,1920]{1,0:T(8,128)} %east_in.1, f32[32,1920]{1,0:T(8,128)} %south_in.1, f32[1,128]{1,0:T(1,128)} %bitcast.12, s32[4,128]{1,0:T(4,128)} %cells.1), custom_call_target="tpu_custom_call" | custom-call | tf_op jit(solution)/shard_map/pack/pallas_call | solution.py:540
  2.5 0.1 collective-permute-done.1
  2.6 0.0 collective-permute-done.cells.partner_cells
  2.6 3.3 %collective-permute-start.2 = (f32[5,4,2048]{2,1,0:T(4,128)S(1)}, f32[5,4,2048]{2,1,0:T(4,128)S(1)}, u32[]{:S(2)}, u32[]{:S(2)}) collective-permute-start(f32[5,4,2048]{2,1,0:T(4,128)S(1)} %join.1), channel_id=1, source_target_pairs={{1,2},{2,1},{3,4},{4,3},{5,6},{6,5},{7,8},{8,7},{9,10},{10,9},{11,... | collective-permute-start | bytes 491528 | tf_op jit(solution)/shard_map/ppermute | solution.py:38
  6.0 1.4 %load.1 = (f32[5,4,1920]{2,1,0:T(4,128)S(1)}, f32[40,1920]{1,0:T(8,128)S(1)}, f32[40,1920]{1,0:T(8,128)S(1)}, f32[40,1920]{1,0:T(8,128)S(1)}, f32[40,1920]{1,0:T(8,128)S(1)}, /*index=5*/s32[32,1920]{1,0:T(8,128)S(1)}) custom-call(f32[32,1920]{1,0:T(8,128)} %depth_in.1, f32[32,1920]{1,0:T(8,128)} %east_in.1, f32[32,1920]{1,0:T(8,128)} %south_in.1, ...), custom_call_target="tpu_custom_call" | custom-call | tf_op jit(solution)/shard_map/load/pallas_call | solution.py:569
  7.4 0.1 collective-permute-start.4
  7.5 0.0 copy-start
  7.5 0.6 %copy-done = f32[8]{0:T(128)S(1)} copy-done((f32[8]{0:T(128)S(1)}, f32[8]{0:T(128)}, u32[]{:S(2)}) %copy-start) | copy-done | bytes 56
  8.2 1.3 %prepare.1 = (f32[40,1920]{1,0:T(8,128)S(1)}, f32[40,1920]{1,0:T(8,128)S(1)}, f32[40,1920]{1,0:T(8,128)S(1)}, f32[40,1920]{1,0:T(8,128)S(1)}, f32[40,1920]{1,0:T...) custom-call(f32[8]{0:T(128)S(1)} %copy-done, ...), custom_call_target="tpu_custom_call", output_to_operand_aliasing={{0}: (5, {}), {1}: (6, {}), {2}: (7, {}), {3}: (8, {})} | custom-call | tf_op jit(solution)/shard_map/prepare/pallas_call | solution.py:579
  9.5 0.8 %collective-permute-done.2.by_other = f32[5,4,2048]{2,1,0:T(4,128)S(1)} collective-permute-done((f32[5,4,2048]{2,1,0:T(4,128)S(1)}, f32[5,4,2048]{2,1,0:T(4,128)S(1)}, u32[]{:S(2)}, u32[]{:S(2)}) %collective-permute-start.2) | collective-permute-done | bytes 163872 | tf_op jit(solution)/shard_map/ppermute | solution.py:38
  10.3 1.1 %collective-permute-start.3 = (f32[2,128]{1,0:T(2,128)S(1)}, f32[2,128]{1,0:T(2,128)S(1)}, u32[]{:S(2)}, u32[]{:S(2)}) collective-permute-start(f32[2,128]{1,0:T(2,128)S(1)} %relay.1.near), channel_id=1, source_target_pairs={{0,1},{1,0},{2,3},{3,2},{4,5},{5,4},{6,7},{7,6},{8,9},{9,8},{10,11... | collective-permute-start | bytes 3080 | tf_op jit(solution)/shard_map/ppermute | solution.py:38
  11.3 0.0 collective-permute-done.4.by_partner
  11.3 0.5 %border.1 = (f32[40,1920]{1,0:T(8,128)S(1)}, f32[40,1920]{1,0:T(8,128)S(1)}, f32[40,1920]{1,0:T(8,128)S(1)}, f32[40,1920]{1,0:T(8,128)S(1)}, f32[40,1920]{1,0:T(...) custom-call(f32[5,4,1920]{2,1,0:T(4,128)S(1)} %collective-permute-do, ...), custom_call_target="tpu_custom_call", output_to_operand_aliasing={{0}: (3, {}), {1}: (4, {}), {2}: (5, {}), {3}: (6, {}), {4}... | custom-call | tf_op jit(solution)/shard_map/border/pallas_call | solution.py:600
  11.9 0.3 %collective-permute-done.3.far = f32[2,128]{1,0:T(2,128)S(1)} collective-permute-done((f32[2,128]{1,0:T(2,128)S(1)}, f32[2,128]{1,0:T(2,128)S(1)}, u32[]{:S(2)}, u32[]{:S(2)}) %collective-permute-start.3) | collective-permute-done | bytes 1056 | tf_op jit(solution)/shard_map/ppermute | solution.py:38
  12.2 9.1 %steps.1 = (f32[1,128]{1,0:T(1,128)S(1)}, f32[1,128]{1,0:T(1,128)S(1)}, f32[1,128]{1,0:T(1,128)S(1)}, f32[40,1920]{1,0:T(8,128)S(1)}, f32[40,1920]{1,0:T(8,128)S...) custom-call(f32[2,128]{1,0:T(2,128)S(1)} %get-tuple-element.49.own, ...), custom_call_target="tpu_custom_call", output_to_operand_aliasing={{3}: (4, {}), {4}: (5, {}), {5}: (6, {}), {6}: (7, {}), {7}... | custom-call | tf_op jit(solution)/shard_map/steps/pallas_call | solution.py:610
  21.2 0.4 %collective-permute-start.5 = (f32[128]{0:T(128)S(1)}, f32[128]{0:T(128)S(1)}, u32[]{:S(2)}, u32[]{:S(2)}) collective-permute-start(f32[128]{0:T(128)S(1)} %bitcast.11), channel_id=1, source_target_pairs={{0,1},{1,0},{2,3},{3,2},{4,5},{5,4},{6,7},{7,6},{8,9},{9,8},{10,11... | collective-permute-start | bytes 1544 | tf_op jit(solution)/shard_map/ppermute | solution.py:38
  21.6 3.2 %collective-permute-start.6 = (f32[128]{0:T(128)S(1)}, f32[128]{0:T(128)S(1)}, u32[]{:S(2)}, u32[]{:S(2)}) collective-permute-start(f32[128]{0:T(128)S(1)} %bitcast.10), channel_id=1, source_target_pairs={{1,2},{2,1},{3,4},{4,3},{5,6},{6,5},{7,8},{8,7},{9,10},{10,9},{11,... | collective-permute-start | bytes 1544 | tf_op jit(solution)/shard_map/ppermute | solution.py:38
  24.8 1.8 %last.1 = (f32[32,1920]{1,0:T(8,128)}, f32[32,1920]{1,0:T(8,128)}, f32[32,1920]{1,0:T(8,128)}) custom-call(f32[40,1920]{1,0:T(8,128)S(1)} %get-tuple-element.78.refs_0_, f32[40,1920]{1,0:T(8,128)S(1)} %get-tuple-element.79.refs_1_, f32[40,1920]{1,0:T(8,128)S(1)} %get-tuple-element.80.refs_2_, f32[40,1920]{1,0:T(8,128)S(1)} %get-tuple-element.81.refs_3_, ...), custom_call_target="tpu_custom_call" | custom-call | tf_op jit(solution)/shard_map/last/pallas_call | solution.py:627
  26.6 0.0 collective-permute-done.5
  26.6 0.7 %collective-permute-done.6 = f32[128]{0:T(128)S(1)} collective-permute-done((f32[128]{0:T(128)S(1)}, f32[128]{0:T(128)S(1)}, u32[]{:S(2)}, u32[]{:S(2)}) %collective-permute-start.6) | collective-permute-done | bytes 544 | tf_op jit(solution)/shard_map/ppermute | solution.py:38
  27.4 0.5 %fusion = f32[128]{0:T(128)} fusion(f32[128]{0:T(128)S(1)} %collective-permute-done.6, f32[128]{0:T(128)S(1)} %collective-permute-done.5, f32[1,128]{1,0:T(1,128)S(1)} %get-tuple-element.91), kind=kLoop, calls=%fused_computation.1 | loop fusion | flops 256 | bytes 2048 | tf_op jit(solution)/shard_map/add | solution.py:637
  (2 shorter events, 0.0 us)
Async XLA Ops:
  0.6 2.0 %collective-permute-start = (s32[4,128]{1,0:T(4,128)}, s32[4,128]{1,0:T(4,128)S(1)}, u32[]{:S(2)}, u32[]{:S(2)}) collective-permute-start(s32[4,128]{1,0:T(4,128)} %cells.1), channel_id=1, source_target_pairs={{0,1},{1,0},{2,3},{3,2},{4,5},{5,4},{6,7},{7,6},{8,9},{9,8},{10,11... | collective-permute-start | bytes 6152 | tf_op jit(solution)/shard_map/ppermute | solution.py:38
  1.4 1.3 %collective-permute-start.1 = (f32[128]{0:T(128)}, f32[128]{0:T(128)S(1)}, u32[]{:S(2)}, u32[]{:S(2)}) collective-permute-start(f32[128]{0:T(128)} %param.11), channel_id=1, source_target_pairs={{0,1},{1,0},{2,3},{3,2},{4,5},{5,4},{6,7},{7,6},{8,9},{9,8},{10,11... | collective-permute-start | bytes 1544 | tf_op jit(solution)/shard_map/ppermute | solution.py:38
  2.6 7.6 %collective-permute-start.2 = (f32[5,4,2048]{2,1,0:T(4,128)S(1)}, f32[5,4,2048]{2,1,0:T(4,128)S(1)}, u32[]{:S(2)}, u32[]{:S(2)}) collective-permute-start(f32[5,4,2048]{2,1,0:T(4,128)S(1)} %join.1), channel_id=1, source_target_pairs={{1,2},{2,1},{3,4},{4,3},{5,6},{6,5},{7,8},{8,7},{9,10},{10,9},{11,... | collective-permute-start | bytes 491528 | tf_op jit(solution)/shard_map/ppermute | solution.py:38
  7.4 3.9 %collective-permute-start.4 = (f32[5,4,1920]{2,1,0:T(4,128)S(1)}, f32[5,4,1920]{2,1,0:T(4,128)S(1)}, u32[]{:S(2)}, u32[]{:S(2)}) collective-permute-start(f32[5,4,1920]{2,1,0:T(4,128)S(1)} %get-tuple-element.57), channel_id=1, source_target_pairs={{0,1},{1,0},{2,3},{3,2},{4,5},{5,4},{6,7},{7,6},{8,9},{9,8},{10,11... | collective-permute-start | bytes 460808 | tf_op jit(solution)/shard_map/ppermute | solution.py:38
  7.5 0.7 %copy-start = (f32[8]{0:T(128)S(1)}, f32[8]{0:T(128)}, u32[]{:S(2)}) copy-start(f32[8]{0:T(128)} %table.1) | copy-start | bytes 100
  10.3 1.9 %collective-permute-start.3 = (f32[2,128]{1,0:T(2,128)S(1)}, f32[2,128]{1,0:T(2,128)S(1)}, u32[]{:S(2)}, u32[]{:S(2)}) collective-permute-start(f32[2,128]{1,0:T(2,128)S(1)} %relay.1.near), channel_id=1, source_target_pairs={{0,1},{1,0},{2,3},{3,2},{4,5},{5,4},{6,7},{7,6},{8,9},{9,8},{10,11... | collective-permute-start | bytes 3080 | tf_op jit(solution)/shard_map/ppermute | solution.py:38
  21.2 5.4 %collective-permute-start.5 = (f32[128]{0:T(128)S(1)}, f32[128]{0:T(128)S(1)}, u32[]{:S(2)}, u32[]{:S(2)}) collective-permute-start(f32[128]{0:T(128)S(1)} %bitcast.11), channel_id=1, source_target_pairs={{0,1},{1,0},{2,3},{3,2},{4,5},{5,4},{6,7},{7,6},{8,9},{9,8},{10,11... | collective-permute-start | bytes 1544 | tf_op jit(solution)/shard_map/ppermute | solution.py:38
  21.6 5.7 %collective-permute-start.6 = (f32[128]{0:T(128)S(1)}, f32[128]{0:T(128)S(1)}, u32[]{:S(2)}, u32[]{:S(2)}) collective-permute-start(f32[128]{0:T(128)S(1)} %bitcast.10), channel_id=1, source_target_pairs={{1,2},{2,1},{3,4},{4,3},{5,6},{6,5},{7,8},{8,7},{9,10},{10,9},{11,... | collective-permute-start | bytes 1544 | tf_op jit(solution)/shard_map/ppermute | solution.py:38

commit v2 on v0

--- a/solution.py
+++ b/solution.py
@@ -202,6 +202,12 @@
             to_partner[slot, :, at] = jnp.where(even, last[8 - HALO :], first[:HALO])
 
 
+def relay_kernel(by_other, prepared, near):
+    del prepared
+    columns = by_other.shape[2] - LANES
+    near[...] = by_other[0, 0:2, columns:]
+
+
 def prepare_kernel(table, rough, own, partner_section, partner_cells, *refs):
     surf, east, south, bed = refs[4:8]
     mann, bed_e, bed_s, drag_e, drag_s, number, total, table_rows = refs[8:]
@@ -324,46 +330,33 @@
     rows = ext - 2 * HALO
     chunks = columns // LANES
     tall = rows if last else ext
-    lane = lanes_of(ext)
+    reach = 2 if last else corridor
+    lane = lanes_of(tall)
     zero = jnp.zeros((tall, LANES), jnp.float32)
-    surfs, rolls, lefts, pairs, turned = {}, {}, {}, {}, {}
-
-    def fetch(chunk):
-        if chunk < chunks:
-            surfs[chunk] = surf[:, cols(chunk)]
-            rolls[chunk] = pltpu.roll(surfs[chunk], LANES - 1, 1)
-        else:
-            rolls[chunk] = rolls[chunks - 1]
-
-    def join(chunk):
-        if chunk < chunks:
-            lefts[chunk] = jnp.where(lane >= LANES - 1, rolls[chunk + 1], rolls[chunk])
-            if not last:
-                pairs[chunk] = surfs[chunk] + lefts[chunk]
-                turned[chunk] = pltpu.roll(pairs[chunk], LANES - 2, 1)
-        else:
-            turned[chunk] = turned.get(chunks - 1)
-
-    fetch(0)
-    fetch(1)
-    join(0)
+
+    def turned(value):
+        return [pltpu.roll(value[:tall], LANES - by, 1) for by in range(1, reach)]
+
+    s0 = surf[:, cols(0)]
+    rolled = turned(s0)
     east_last = zero
     state = (zero, zero)
     for chunk in range(chunks):
         at = cols(chunk)
-        if not last:
-            if chunk + 2 <= chunks:
-                fetch(chunk + 2)
-            join(chunk + 1)
-        elif chunk > 0:
-            fetch(chunk + 1)
-            join(chunk)
-        s0 = surfs[chunk]
+        if chunk + 1 < chunks:
+            s1 = surf[:, cols(chunk + 1)]
+            rolled_then = turned(s1)
+        else:
+            s1, rolled_then = s0, rolled
+        moved = [
+            jnp.where(lane >= LANES - 1 - by, rolled_then[by], rolled[by])
+            for by in range(reach - 1)
+        ]
         if fluxes_done:
             new_east, new_south = east[:, at], south[:, at]
         else:
             new_east = face(
-                east[:tall, at], s0[:tall], lefts[chunk][:tall], bed_e[:tall, at], drag_e[:tall, at]
+                east[:tall, at], s0[:tall], moved[0], bed_e[:tall, at], drag_e[:tall, at]
             )
             new_east = east_walled(new_east, chunk, chunks)
             new_south = face(south[:, at], s0, moved_up(s0), bed_s[:, at], drag_s[:, at])
@@ -372,21 +365,19 @@
             )
         held = total[:tall, at]
         summed, state = right_sum(held, state)
+        new_total = None
         if not last:
-            window = pairs[chunk] + jnp.where(
-                lane >= LANES - 2, turned[chunk + 1], turned[chunk]
-            )
-            total[:, at] = (1.0 - corridor * DRAIN) * held + count[:, at] * window
+            window = (s0 + moved[0]) + sum(moved[2:], moved[1])
+            new_total = (1.0 - corridor * DRAIN) * held + count[:, at] * window
         east_rolled = pltpu.roll(new_east, 1, 1)
         north = pltpu.roll(new_south, 1, 0)
-        inflow = jnp.where(lane[:tall] < 1, east_last, east_rolled) + north[:tall]
+        inflow = jnp.where(lane < 1, east_last, east_rolled) + north[:tall]
         east_last = east_rolled
-        new_surf = (
-            s0[:tall]
-            + SPREAD * (inflow - new_east - new_south[:tall])
-            + (summed - covers[:tall, at] * s0[:tall])
-        )
-        yield chunk, new_surf, new_east, new_south
+        outflow = new_east + new_south[:tall]
+        gain = summed - covers[:tall, at] * s0[:tall]
+        new_surf = s0[:tall] + (SPREAD * (inflow - outflow) + gain)
+        yield chunk, new_surf, new_east, new_south, new_total
+        s0, rolled = s1, rolled_then
 
 
 def steps_kernel(corridor, tiles, own, partner_cells, near, far, *refs):
@@ -420,20 +411,16 @@
 
     wall = wall_of(ext, tiles)
     state_refs = (surf, east, south, bed_e, bed_s, drag_e, drag_s, total, covers, count)
-    for chunk, new_surf, new_east, new_south in substep(True, False, corridor, wall, state_refs):
-        surf[:, cols(chunk)] = new_surf
-
-    def body(step, carry):
-        for chunk, new_surf, new_east, new_south in substep(
-            False, False, corridor, wall, state_refs
+    for step in range(STEPS - 1):
+        for chunk, new_surf, new_east, new_south, new_total in substep(
+            step == 0, False, corridor, wall, state_refs
         ):
             at = cols(chunk)
             surf[:, at] = new_surf
-            east[:, at] = new_east
-            south[:, at] = new_south
-        return carry
-
-    lax.fori_loop(0, STEPS - 2, body, 0)
+            total[:, at] = new_total
+            if step > 0:
+                east[:, at] = new_east
+                south[:, at] = new_south
 
     kept = (1.0 - corridor * DRAIN) ** STEPS
     levels = []
@@ -476,7 +463,7 @@
     group = 5
     copies = []
     steps = substep(False, True, corridor, wall_of(ext, tiles), refs[:9] + (None,))
-    for chunk, new_surf, new_east, new_south in steps:
+    for chunk, new_surf, new_east, new_south, _ in steps:
         at = cols(chunk)
         results[0][:, at] = new_surf - bed[:rows, at]
         results[1][:, at] = new_east
@@ -568,7 +555,14 @@
         manning_table,
         *[held(value) for value in (rough, own, partner_section, partner_cells, *loaded)],
     )
-    near = by_other[0, 0:2, columns:]
+    near = pl.pallas_call(
+        relay_kernel,
+        out_shape=pltpu.VMEM((2, owned), jnp.float32),
+        in_specs=[VMEM_SPEC] * 2,
+        out_specs=VMEM_SPEC,
+        compiler_params=params,
+        name="relay",
+    )(held(by_other), held(table_rows))
     from_far = swapped(near, 0)
     fields = pl.pallas_call(
         functools.partial(border_kernel, tiles),

time: 27.3 us -> 24.8 us (0.908)
  waiting for transfers between devices: 3.84 us -> 2.17 us
  Pallas kernels: 12.6 us -> 11.6 us
  starting transfers between devices: 8.59 us -> 8.91 us
    ppermute x7, waiting for transfers between devices: 3.84 us -> 2.17 us  [swapped(): return lax.ppermute(value, 'gy', pairs)]
    pallas_call x1, Pallas kernels: 6.7 us -> 5.72 us  [local(): pl.pallas_call(functools.partial(steps_kernel, corridor, tiles), out_shap...]
    ppermute x7, starting transfers between devices: 8.59 us -> 8.91 us  [swapped(): return lax.ppermute(value, 'gy', pairs)]
  transfers between devices with their start and end apart: 7 -> 7, of which waited for: 3 -> 4; matrix products, arithmetic and copies ran while one was open for 0% -> 0% of each run, Pallas kernels for 22% -> 24%
where the time goes in v2:
time: 24.8 us; the launch traced here: 24.5 us
  Pallas kernels  11.6 us (47%)
  starting transfers between devices  8.91 us (36%)
  waiting for transfers between devices  2.17 us (9%)
  between operations  0.72 us (3%)
  local copies, waits for them, and re-layouts  0.65 us (3%)
  other arithmetic  0.51 us (2%)
    ppermute x7, starting transfers between devices, swapped(): return lax.ppermute(value, 'gy', pairs)  8.91 us
    pallas_call x1, Pallas kernels, local(): pl.pallas_call(functools.partial(steps_kernel, corridor, tiles), out_shap...  5.72 us
    ppermute x7, waiting for transfers between devices, swapped(): return lax.ppermute(value, 'gy', pairs)  2.17 us
    pallas_call x1, Pallas kernels, local(): pl.pallas_call(functools.partial(last_kernel, corridor, tiles), out_shape...  1.59 us
    pallas_call x1, Pallas kernels, local(): pl.pallas_call(load_kernel, out_shape=[halo] + [field] * 4 + [pltpu.VMEM(...  1.44 us
    pallas_call x1, Pallas kernels, local(): pl.pallas_call(prepare_kernel, out_shape=[field] * 11 + [pltpu.VMEM((mann...  1.27 us
    pallas_call x1, Pallas kernels, local(): pl.pallas_call(pack_kernel, out_shape=[wide, pltpu.VMEM((2, owned), jnp.f...  1.02 us
    unnamed x2, local copies, waits for them, and re-layouts  0.65 us
  transfers between devices with their start and end apart: 7, of which 4 were waited for; matrix products, arithmetic and copies ran while one was open for 0% of the time, Pallas kernels for 24%

profile of v2, /device:TPU:7, one launch (start us, length us, event | category | flops | bytes accessed | tf_op | source)
XLA Modules:
  0.0 24.5 jit_solution(8929865681616243511)
XLA Ops:
  0.6 0.7 %collective-permute-start = (s32[4,128]{1,0:T(4,128)}, s32[4,128]{1,0:T(4,128)S(1)}, u32[]{:S(2)}, u32[]{:S(2)}) collective-permute-start(s32[4,128]{1,0:T(4,128)} %cells.1), channel_id=1, source_target_pairs={{0,1},{1,0},{2,3},{3,2},{4,5},{5,4},{6,7},{7,6},{8,9},{9,8},{10,11... | collective-permute-start | bytes 6152 | tf_op jit(solution)/shard_map/ppermute | solution.py:38
  1.4 0.1 collective-permute-start.1
  1.4 1.0 %pack.1 = (f32[5,4,2048]{2,1,0:T(4,128)S(1)}, f32[2,128]{1,0:T(2,128)S(1)}) custom-call(f32[32,1920]{1,0:T(8,128)} %depth_in.1, f32[32,1920]{1,0:T(8,128)} %bed_in.1, s32[32,1920]{1,0:T(8,128)} %rough_in.1, f32[32,1920]{1,0:T(8,128)} %east_in.1, f32[32,1920]{1,0:T(8,128)} %south_in.1, f32[1,128]{1,0:T(1,128)} %bitcast.12, s32[4,128]{1,0:T(4,128)} %cells.1), custom_call_target="tpu_custom_call" | custom-call | tf_op jit(solution)/shard_map/pack/pallas_call | solution.py:507
  2.5 0.1 collective-permute-done.1
  2.6 0.0 collective-permute-done.cells.partner_cells
  2.6 3.3 %collective-permute-start.2 = (f32[5,4,2048]{2,1,0:T(4,128)S(1)}, f32[5,4,2048]{2,1,0:T(4,128)S(1)}, u32[]{:S(2)}, u32[]{:S(2)}) collective-permute-start(f32[5,4,2048]{2,1,0:T(4,128)S(1)} %join.1), channel_id=1, source_target_pairs={{1,2},{2,1},{3,4},{4,3},{5,6},{6,5},{7,8},{8,7},{9,10},{10,9},{11,... | collective-permute-start | bytes 491528 | tf_op jit(solution)/shard_map/ppermute | solution.py:38
  6.0 1.4 %load.1 = (f32[5,4,1920]{2,1,0:T(4,128)S(1)}, f32[40,1920]{1,0:T(8,128)S(1)}, f32[40,1920]{1,0:T(8,128)S(1)}, f32[40,1920]{1,0:T(8,128)S(1)}, f32[40,1920]{1,0:T(8,128)S(1)}, /*index=5*/s32[32,1920]{1,0:T(8,128)S(1)}) custom-call(f32[32,1920]{1,0:T(8,128)} %depth_in.1, f32[32,1920]{1,0:T(8,128)} %east_in.1, f32[32,1920]{1,0:T(8,128)} %south_in.1, ...), custom_call_target="tpu_custom_call" | custom-call | tf_op jit(solution)/shard_map/load/pallas_call | solution.py:536
  7.4 0.1 collective-permute-start.4
  7.5 0.0 copy-start
  7.5 0.6 %copy-done = f32[8]{0:T(128)S(1)} copy-done((f32[8]{0:T(128)S(1)}, f32[8]{0:T(128)}, u32[]{:S(2)}) %copy-start) | copy-done | bytes 56
  8.2 1.3 %prepare.1 = (f32[40,1920]{1,0:T(8,128)S(1)}, f32[40,1920]{1,0:T(8,128)S(1)}, f32[40,1920]{1,0:T(8,128)S(1)}, f32[40,1920]{1,0:T(8,128)S(1)}, f32[40,1920]{1,0:T...) custom-call(f32[8]{0:T(128)S(1)} %copy-done, ...), custom_call_target="tpu_custom_call", output_to_operand_aliasing={{0}: (5, {}), {1}: (6, {}), {2}: (7, {}), {3}: (8, {})} | custom-call | tf_op jit(solution)/shard_map/prepare/pallas_call | solution.py:546
  9.5 0.8 %collective-permute-done.2.by_other = f32[5,4,2048]{2,1,0:T(4,128)S(1)} collective-permute-done((f32[5,4,2048]{2,1,0:T(4,128)S(1)}, f32[5,4,2048]{2,1,0:T(4,128)S(1)}, u32[]{:S(2)}, u32[]{:S(2)}) %collective-permute-start.2) | collective-permute-done | bytes 163872 | tf_op jit(solution)/shard_map/ppermute | solution.py:38
  10.3 1.1 %collective-permute-start.3 = (f32[2,128]{1,0:T(2,128)S(1)}, f32[2,128]{1,0:T(2,128)S(1)}, u32[]{:S(2)}, u32[]{:S(2)}) collective-permute-start(f32[2,128]{1,0:T(2,128)S(1)} %relay.1.near), channel_id=1, source_target_pairs={{0,1},{1,0},{2,3},{3,2},{4,5},{5,4},{6,7},{7,6},{8,9},{9,8},{10,11... | collective-permute-start | bytes 3080 | tf_op jit(solution)/shard_map/ppermute | solution.py:38
  11.3 0.0 collective-permute-done.4.by_partner
  11.3 0.5 %border.1 = (f32[40,1920]{1,0:T(8,128)S(1)}, f32[40,1920]{1,0:T(8,128)S(1)}, f32[40,1920]{1,0:T(8,128)S(1)}, f32[40,1920]{1,0:T(8,128)S(1)}, f32[40,1920]{1,0:T(...) custom-call(f32[5,4,1920]{2,1,0:T(4,128)S(1)} %collective-permute-do, ...), custom_call_target="tpu_custom_call", output_to_operand_aliasing={{0}: (3, {}), {1}: (4, {}), {2}: (5, {}), {3}: (6, {}), {4}... | custom-call | tf_op jit(solution)/shard_map/border/pallas_call | solution.py:567
  11.9 0.3 %collective-permute-done.3.far = f32[2,128]{1,0:T(2,128)S(1)} collective-permute-done((f32[2,128]{1,0:T(2,128)S(1)}, f32[2,128]{1,0:T(2,128)S(1)}, u32[]{:S(2)}, u32[]{:S(2)}) %collective-permute-start.3) | collective-permute-done | bytes 1056 | tf_op jit(solution)/shard_map/ppermute | solution.py:38
  12.2 5.7 %steps.1 = (f32[1,128]{1,0:T(1,128)S(1)}, f32[1,128]{1,0:T(1,128)S(1)}, f32[1,128]{1,0:T(1,128)S(1)}, f32[40,1920]{1,0:T(8,128)S(1)}, f32[40,1920]{1,0:T(8,128)S...) custom-call(f32[2,128]{1,0:T(2,128)S(1)} %get-tuple-element.49.own, ...), custom_call_target="tpu_custom_call", output_to_operand_aliasing={{3}: (4, {}), {4}: (5, {}), {5}: (6, {}), {6}: (7, {}), {7}... | custom-call | tf_op jit(solution)/shard_map/steps/pallas_call | solution.py:577
  17.9 0.4 %collective-permute-start.5 = (f32[128]{0:T(128)S(1)}, f32[128]{0:T(128)S(1)}, u32[]{:S(2)}, u32[]{:S(2)}) collective-permute-start(f32[128]{0:T(128)S(1)} %bitcast.11), channel_id=1, source_target_pairs={{0,1},{1,0},{2,3},{3,2},{4,5},{5,4},{6,7},{7,6},{8,9},{9,8},{10,11... | collective-permute-start | bytes 1544 | tf_op jit(solution)/shard_map/ppermute | solution.py:38
  18.3 3.2 %collective-permute-start.6 = (f32[128]{0:T(128)S(1)}, f32[128]{0:T(128)S(1)}, u32[]{:S(2)}, u32[]{:S(2)}) collective-permute-start(f32[128]{0:T(128)S(1)} %bitcast.10), channel_id=1, source_target_pairs={{1,2},{2,1},{3,4},{4,3},{5,6},{6,5},{7,8},{8,7},{9,10},{10,9},{11,... | collective-permute-start | bytes 1544 | tf_op jit(solution)/shard_map/ppermute | solution.py:38
  21.5 1.6 %last.1 = (f32[32,1920]{1,0:T(8,128)}, f32[32,1920]{1,0:T(8,128)}, f32[32,1920]{1,0:T(8,128)}) custom-call(f32[40,1920]{1,0:T(8,128)S(1)} %get-tuple-element.78.refs_0_, f32[40,1920]{1,0:T(8,128)S(1)} %get-tuple-element.79.refs_1_, f32[40,1920]{1,0:T(8,128)S(1)} %get-tuple-element.80.refs_2_, f32[40,1920]{1,0:T(8,128)S(1)} %get-tuple-element.81.refs_3_, ...), custom_call_target="tpu_custom_call" | custom-call | tf_op jit(solution)/shard_map/last/pallas_call | solution.py:594
  23.1 0.0 collective-permute-done.5
  23.1 0.9 %collective-permute-done.6 = f32[128]{0:T(128)S(1)} collective-permute-done((f32[128]{0:T(128)S(1)}, f32[128]{0:T(128)S(1)}, u32[]{:S(2)}, u32[]{:S(2)}) %collective-permute-start.6) | collective-permute-done | bytes 544 | tf_op jit(solution)/shard_map/ppermute | solution.py:38
  24.0 0.5 %fusion = f32[128]{0:T(128)} fusion(f32[128]{0:T(128)S(1)} %collective-permute-done.6, f32[128]{0:T(128)S(1)} %collective-permute-done.5, f32[1,128]{1,0:T(1,128)S(1)} %get-tuple-element.91), kind=kLoop, calls=%fused_computation.1 | loop fusion | flops 256 | bytes 2048 | tf_op jit(solution)/shard_map/add | solution.py:604
  (2 shorter events, 0.0 us)
Async XLA Ops:
  0.6 2.0 %collective-permute-start = (s32[4,128]{1,0:T(4,128)}, s32[4,128]{1,0:T(4,128)S(1)}, u32[]{:S(2)}, u32[]{:S(2)}) collective-permute-start(s32[4,128]{1,0:T(4,128)} %cells.1), channel_id=1, source_target_pairs={{0,1},{1,0},{2,3},{3,2},{4,5},{5,4},{6,7},{7,6},{8,9},{9,8},{10,11... | collective-permute-start | bytes 6152 | tf_op jit(solution)/shard_map/ppermute | solution.py:38
  1.4 1.3 %collective-permute-start.1 = (f32[128]{0:T(128)}, f32[128]{0:T(128)S(1)}, u32[]{:S(2)}, u32[]{:S(2)}) collective-permute-start(f32[128]{0:T(128)} %param.11), channel_id=1, source_target_pairs={{0,1},{1,0},{2,3},{3,2},{4,5},{5,4},{6,7},{7,6},{8,9},{9,8},{10,11... | collective-permute-start | bytes 1544 | tf_op jit(solution)/shard_map/ppermute | solution.py:38
  2.6 7.6 %collective-permute-start.2 = (f32[5,4,2048]{2,1,0:T(4,128)S(1)}, f32[5,4,2048]{2,1,0:T(4,128)S(1)}, u32[]{:S(2)}, u32[]{:S(2)}) collective-permute-start(f32[5,4,2048]{2,1,0:T(4,128)S(1)} %join.1), channel_id=1, source_target_pairs={{1,2},{2,1},{3,4},{4,3},{5,6},{6,5},{7,8},{8,7},{9,10},{10,9},{11,... | collective-permute-start | bytes 491528 | tf_op jit(solution)/shard_map/ppermute | solution.py:38
  7.4 3.9 %collective-permute-start.4 = (f32[5,4,1920]{2,1,0:T(4,128)S(1)}, f32[5,4,1920]{2,1,0:T(4,128)S(1)}, u32[]{:S(2)}, u32[]{:S(2)}) collective-permute-start(f32[5,4,1920]{2,1,0:T(4,128)S(1)} %get-tuple-element.57), channel_id=1, source_target_pairs={{0,1},{1,0},{2,3},{3,2},{4,5},{5,4},{6,7},{7,6},{8,9},{9,8},{10,11... | collective-permute-start | bytes 460808 | tf_op jit(solution)/shard_map/ppermute | solution.py:38
  7.5 0.7 %copy-start = (f32[8]{0:T(128)S(1)}, f32[8]{0:T(128)}, u32[]{:S(2)}) copy-start(f32[8]{0:T(128)} %table.1) | copy-start | bytes 100
  10.3 1.9 %collective-permute-start.3 = (f32[2,128]{1,0:T(2,128)S(1)}, f32[2,128]{1,0:T(2,128)S(1)}, u32[]{:S(2)}, u32[]{:S(2)}) collective-permute-start(f32[2,128]{1,0:T(2,128)S(1)} %relay.1.near), channel_id=1, source_target_pairs={{0,1},{1,0},{2,3},{3,2},{4,5},{5,4},{6,7},{7,6},{8,9},{9,8},{10,11... | collective-permute-start | bytes 3080 | tf_op jit(solution)/shard_map/ppermute | solution.py:38
  17.9 5.2 %collective-permute-start.5 = (f32[128]{0:T(128)S(1)}, f32[128]{0:T(128)S(1)}, u32[]{:S(2)}, u32[]{:S(2)}) collective-permute-start(f32[128]{0:T(128)S(1)} %bitcast.11), channel_id=1, source_target_pairs={{0,1},{1,0},{2,3},{3,2},{4,5},{5,4},{6,7},{7,6},{8,9},{9,8},{10,11... | collective-permute-start | bytes 1544 | tf_op jit(solution)/shard_map/ppermute | solution.py:38
  18.3 5.7 %collective-permute-start.6 = (f32[128]{0:T(128)S(1)}, f32[128]{0:T(128)S(1)}, u32[]{:S(2)}, u32[]{:S(2)}) collective-permute-start(f32[128]{0:T(128)S(1)} %bitcast.10), channel_id=1, source_target_pairs={{1,2},{2,1},{3,4},{4,3},{5,6},{6,5},{7,8},{8,7},{9,10},{10,9},{11,... | collective-permute-start | bytes 1544 | tf_op jit(solution)/shard_map/ppermute | solution.py:38

commit v3 on v2

--- a/solution.py
+++ b/solution.py
@@ -173,6 +173,22 @@
     to_other[0, 3:4, columns:] = (cells[0:1, :] + 1).astype(jnp.float32)
 
 
+def picking(key, lane, takes, at_lane):
+    for block in range(key.shape[1] // LANES):
+        mine = slice(block * LANES, (block + 1) * LANES)
+
+        def column(row):
+            wide = jnp.broadcast_to(row[:, mine].astype(jnp.float32), (LANES, LANES))
+            return jnp.transpose(wide).astype(jnp.int32)
+
+        spread = lanes_of(LANES)
+        at = column(key)
+        for first in range(0, takes.shape[1], LANES):
+            hit = jnp.where(spread + first == at, 1.0, 0.0)
+            takes[mine, first : first + LANES] = hit.astype(jnp.bfloat16)
+        at_lane[mine, :] = jnp.where(spread == column(lane), 1.0, 0.0)
+
+
 def load_kernel(
     depth_in, east_in, south_in, bed_in, rough_in, to_partner, surf, east, south, bed, rough, sems
 ):
@@ -210,7 +226,7 @@
 
 def prepare_kernel(table, rough, own, partner_section, partner_cells, *refs):
     surf, east, south, bed = refs[4:8]
-    mann, bed_e, bed_s, drag_e, drag_s, number, total, table_rows = refs[8:]
+    mann, bed_e, bed_s, drag_e, drag_s, number, total, table_rows, takes, at_lane = refs[8:]
     ext, columns = surf.shape
     rows = ext - 2 * HALO
     chunks = columns // LANES
@@ -235,6 +251,9 @@
         at = cols(chunk)
         number[:, at] = starts[chunk * ext : (chunk + 1) * ext]
         total[:, at] = levels[chunk * ext : (chunk + 1) * ext]
+
+    key = jnp.where(valid & (node_row < rows), node_chunk * rows + node_row, -1)
+    picking(key, node_lane, takes, at_lane)
 
     kept = lax.broadcasted_iota(jnp.int32, (rows, LANES), 0) == rows - 1
     for chunk in range(chunks):
@@ -264,7 +283,7 @@
 
 
 def border_kernel(tiles, by_partner, by_other, table_rows, *refs):
-    surf, east, south, bed, mann, bed_e, bed_s, drag_e, drag_s, number, total = refs[11:]
+    surf, east, south, bed, mann, bed_e, bed_s, drag_e, drag_s, number, total, takes, at_lane = refs[11:]
     ext, columns = surf.shape
     rows = ext - 2 * HALO
     chunks = columns // LANES
@@ -291,6 +310,9 @@
     valid, node_row, node_chunk, node_lane = located(cell, position, rows, ext, columns)
     key = jnp.where(valid, node_chunk * ext + node_row, -1)
     starts, levels = scattered(section, key, node_lane, chunks * ext)
+
+    key = jnp.where(valid & (node_row < rows), node_chunk * rows + node_row, -1)
+    picking(key[:, :LANES], node_lane[:, :LANES], takes, at_lane)
 
     wall = wall_of(ext, tiles)
     kept = lax.broadcasted_iota(jnp.int32, (16, LANES), 0) < 7
@@ -380,17 +402,17 @@
         s0, rolled = s1, rolled_then
 
 
-def steps_kernel(corridor, tiles, own, partner_cells, near, far, *refs):
-    number = refs[7]
-    own_term, partner_term, other_term = refs[9:12]
-    surf, east, south, bed_e, bed_s, drag_e, drag_s, total, covers = refs[12:21]
-    count, first_total = refs[21:]
+def steps_kernel(corridor, tiles, own, far, *refs):
+    surf, east, south, bed_e, bed_s, drag_e, drag_s, number, total = refs[:9]
+    takes, at_lane, takes_near, at_lane_near = refs[9:13]
+    own_term, partner_term, other_term = refs[13:16]
+    surf_out, east_out, south_out, total_out, covers = refs[16:21]
+    count, total_0, total_1, total_2, surf_1, surf_2, east_1, south_1 = refs[21:]
     ext, columns = surf.shape
     rows = ext - 2 * HALO
     owned = own.shape[1]
     chunks = columns // LANES
     position = lax.axis_index("gy")
-    side = jnp.where(position % 2 == 0, 1, -1)
 
     valid, node_row, node_chunk, node_lane = located(far[1:2, :], position, rows, ext, columns)
     key = jnp.where(valid & (node_row >= rows), node_chunk * 8 + (node_row - rows), -1)
@@ -404,49 +426,71 @@
         held = total[:, at]
         held = FEED * jnp.concatenate([held[:rows], held[rows:] + levels[mine]], axis=0)
         count[:, at] = (FEED * DRAIN) * starting
-        total[:, at] = held
-        first_total[:, at] = held[:rows]
+        total_0[:, at] = held
         covering, state = right_sum(starting, state)
         covers[:, at] = FEED * covering
 
     wall = wall_of(ext, tiles)
-    state_refs = (surf, east, south, bed_e, bed_s, drag_e, drag_s, total, covers, count)
+    faces = (bed_e, bed_s, drag_e, drag_s)
+    befores = (
+        (surf, east, south, total_0),
+        (surf_1, east, south, total_1),
+        (surf_2, east_1, south_1, total_2),
+    )
+    afters = (
+        (surf_1, None, None, total_1),
+        (surf_2, east_1, south_1, total_2),
+        (surf_out, east_out, south_out, total_out),
+    )
     for step in range(STEPS - 1):
-        for chunk, new_surf, new_east, new_south, new_total in substep(
-            step == 0, False, corridor, wall, state_refs
-        ):
-            at = cols(chunk)
-            surf[:, at] = new_surf
-            total[:, at] = new_total
-            if step > 0:
-                east[:, at] = new_east
-                south[:, at] = new_south
+        before, after = befores[step], afters[step]
+        state_refs = (*before[:3], *faces, before[3], covers, count)
+        for chunk, *results in substep(step == 0, False, corridor, wall, state_refs):
+            for target, result in zip(after, results):
+                if target is not None:
+                    target[:, cols(chunk)] = result
 
     kept = (1.0 - corridor * DRAIN) ** STEPS
+    lane = lanes_of(rows)
+
+    def turned(value):
+        return [pltpu.roll(value, LANES - by, 1) for by in range(1, corridor)]
+
+    s0 = surf_out[:rows, cols(0)]
+    rolled = turned(s0)
     levels = []
     for chunk in range(chunks):
-        at, then = cols(chunk), cols(min(chunk + 1, chunks - 1))
-        window = surf[:rows, at]
-        for by in range(1, corridor):
-            window = window + moved_left(surf[:rows, at], surf[:rows, then], by)
+        at = cols(chunk)
+        if chunk + 1 < chunks:
+            s1 = surf_out[:rows, cols(chunk + 1)]
+            rolled_then = turned(s1)
+        else:
+            s1, rolled_then = s0, rolled
+        window = s0
+        for by in range(corridor - 1):
+            window = window + jnp.where(lane >= LANES - 1 - by, rolled_then[by], rolled[by])
         starting = count[:rows, at]
-        held = (1.0 - corridor * DRAIN) * total[:rows, at] + starting * window
-        gained = held - kept * first_total[:, at]
+        held = (1.0 - corridor * DRAIN) * total_out[:rows, at] + starting * window
+        gained = held - kept * total_0[:rows, at]
         weight = jnp.maximum(starting * (1.0 / DRAIN), FEED)
         levels.append(gained * pl.reciprocal(weight, approx=True))
-    partner = jnp.where(position + side < tiles, partner_cells[0:1, :] + 1, 0).astype(jnp.float32)
-    cell = jnp.concatenate([own[1:2, :], partner, near[1:2, :]], axis=1)
-    valid, node_row, node_chunk, node_lane = located(cell, position, rows, ext, columns)
-    take_key = jnp.where(valid & (node_row < rows), node_chunk * rows + node_row, -1)
-    takes = one_hot(chunks * rows, take_key).astype(jnp.bfloat16)
-    picked = lax.dot_general(
+        s0, rolled = s1, rolled_then
+    spare = takes.shape[1] - chunks * rows
+    if spare:
+        levels.append(jnp.zeros((spare, LANES), jnp.float32))
+    picked = jnp.dot(
+        jnp.concatenate([takes[...], takes_near[...]], axis=0),
         jnp.concatenate(split3(jnp.concatenate(levels, axis=0)), axis=1),
-        takes,
-        (((0,), (0,)), ((), ())),
         preferred_element_type=jnp.float32,
     )
-    picked = (picked[:LANES] + picked[LANES : 2 * LANES]) + picked[2 * LANES :]
-    terms = jnp.sum(picked * one_hot(LANES, node_lane), axis=0, keepdims=True)
+    hit = jnp.concatenate([at_lane[...], at_lane_near[...]], axis=0)
+    picked = (picked * jnp.concatenate([hit] * 3, axis=1)).astype(jnp.bfloat16)
+    terms = lax.dot_general(
+        jnp.ones((8, 3 * LANES), jnp.bfloat16),
+        picked,
+        (((1,), (1,)), ((), ())),
+        preferred_element_type=jnp.float32,
+    )[0:1]
     own_term[...] = kept * own[0:1, :] + terms[:, :owned]
     partner_term[...] = terms[:, owned : 2 * owned]
     other_term[...] = terms[:, 2 * owned :]
@@ -503,6 +547,7 @@
     halo = pltpu.VMEM((5, HALO, columns), jnp.float32)
     field = pltpu.VMEM((ext, columns), jnp.float32)
     term = pltpu.VMEM((1, owned), jnp.float32)
+    cells = -(-chunks * rows // LANES) * LANES
     wide = pltpu.VMEM((5, HALO, columns + LANES), jnp.float32)
     to_other, own = pl.pallas_call(
         pack_kernel,
@@ -543,11 +588,16 @@
         name="load",
     )(*[far(value) for value in (depth, flux_east, flux_south, bed_level, rough_class)])
     by_partner = swapped(to_partner, 0)
-    *fields, table_rows = pl.pallas_call(
+    *fields, table_rows, takes, at_lane = pl.pallas_call(
         prepare_kernel,
-        out_shape=[field] * 11 + [pltpu.VMEM((manning_table.shape[0], LANES), jnp.float32)],
+        out_shape=[field] * 11
+        + [
+            pltpu.VMEM((manning_table.shape[0], LANES), jnp.float32),
+            pltpu.VMEM((2 * owned, cells), jnp.bfloat16),
+            pltpu.VMEM((2 * owned, LANES), jnp.float32),
+        ],
         in_specs=[SMEM_SPEC] + [VMEM_SPEC] * 8,
-        out_specs=[VMEM_SPEC] * 12,
+        out_specs=[VMEM_SPEC] * 14,
         input_output_aliases={5 + slot: slot for slot in range(4)},
         compiler_params=params,
         name="prepare",
@@ -564,30 +614,35 @@
         name="relay",
     )(held(by_other), held(table_rows))
     from_far = swapped(near, 0)
-    fields = pl.pallas_call(
+    *fields, takes_near, at_lane_near = pl.pallas_call(
         functools.partial(border_kernel, tiles),
-        out_shape=[field] * 11,
+        out_shape=[field] * 11
+        + [pltpu.VMEM((owned, cells), jnp.bfloat16), pltpu.VMEM((owned, LANES), jnp.float32)],
         in_specs=[VMEM_SPEC] * 14,
-        out_specs=[VMEM_SPEC] * 11,
+        out_specs=[VMEM_SPEC] * 13,
         input_output_aliases={3 + slot: slot for slot in range(11)},
         compiler_params=params,
         name="border",
     )(*[held(value) for value in (by_partner, by_other, table_rows, *fields)])
-    surf, east, south, bed, _, bed_e, bed_s, drag_e, drag_s, number, total = fields
+    surf, east, south, bed, _, *faces, number, total = fields
     stepped = pl.pallas_call(
         functools.partial(steps_kernel, corridor, tiles),
-        out_shape=[term] * 3 + [field] * 9,
-        in_specs=[VMEM_SPEC] * 13,
-        out_specs=[VMEM_SPEC] * 12,
-        scratch_shapes=[field, pltpu.VMEM((rows, columns), jnp.float32)],
-        input_output_aliases={4 + slot: 3 + slot for slot in range(7)} | {12: 10},
+        out_shape=[term] * 3 + [field] * 5,
+        in_specs=[VMEM_SPEC] * 15,
+        out_specs=[VMEM_SPEC] * 8,
+        scratch_shapes=[field] * 8,
         compiler_params=params,
         name="steps",
     )(
-        *[held(value) for value in (own, partner_cells, near, from_far)],
-        *[held(value) for value in (surf, east, south, bed_e, bed_s, drag_e, drag_s)],
-        *[held(value) for value in (number, total)],
-    )
+        *[
+            held(value)
+            for value in (
+                *(own, from_far, surf, east, south, *faces, number, total),
+                *(takes, at_lane, takes_near, at_lane_near),
+            )
+        ]
+    )
+    surf, east, south, total, covers = stepped[3:]
     from_other = swapped(stepped[2].reshape(owned), 1)
     from_partner = swapped(stepped[1].reshape(owned), 0)
     result = pltpu.HBM((rows, columns), jnp.float32)
@@ -600,7 +655,7 @@
         + [pltpu.SemaphoreType.DMA((-(-chunks // 5), 3))],
         compiler_params=params,
         name="last",
-    )(*[held(value) for value in (*stepped[3:], bed)])
+    )(*[held(value) for value in (surf, east, south, *faces, total, covers, bed)])
     river_section = stepped[0].reshape(owned) + from_partner + from_other
     return (depth, flux_east, flux_south, river_section)
 

time: 24.8 us -> 23.8 us (0.960)
  Pallas kernels: 11.6 us -> 10.8 us
    pallas_call x1, Pallas kernels: 5.72 us -> 4.8 us  [local(): pl.pallas_call(functools.partial(steps_kernel, corridor, tiles), out_shap...]
  transfers between devices with their start and end apart: 7 -> 7, of which waited for: 4 -> 4; matrix products, arithmetic and copies ran while one was open for 0% -> 0% of each run, Pallas kernels for 24% -> 25%
where the time goes in v3:
time: 23.8 us; the launch traced here: 23.6 us
  Pallas kernels  10.8 us (45%)
  starting transfers between devices  8.87 us (37%)
  waiting for transfers between devices  2.02 us (8%)
  between operations  0.71 us (3%)
  local copies, waits for them, and re-layouts  0.65 us (3%)
  other arithmetic  0.51 us (2%)
    ppermute x7, starting transfers between devices, swapped(): return lax.ppermute(value, 'gy', pairs)  8.87 us
    pallas_call x1, Pallas kernels, local(): pl.pallas_call(functools.partial(steps_kernel, corridor, tiles), out_shap...  4.8 us
    ppermute x7, waiting for transfers between devices, swapped(): return lax.ppermute(value, 'gy', pairs)  2.02 us
    pallas_call x1, Pallas kernels, local(): pl.pallas_call(functools.partial(last_kernel, corridor, tiles), out_shape...  1.59 us
    pallas_call x1, Pallas kernels, local(): pl.pallas_call(load_kernel, out_shape=[halo] + [field] * 4 + [pltpu.VMEM(...  1.44 us
    pallas_call x1, Pallas kernels, local(): pl.pallas_call(prepare_kernel, out_shape=[field] * 11 + [pltpu.VMEM((mann...  1.39 us
    pallas_call x1, Pallas kernels, local(): pl.pallas_call(pack_kernel, out_shape=[wide, pltpu.VMEM((2, owned), jnp.f...  1.02 us
    unnamed x2, local copies, waits for them, and re-layouts  0.65 us
  transfers between devices with their start and end apart: 7, of which 4 were waited for; matrix products, arithmetic and copies ran while one was open for 0% of the time, Pallas kernels for 25%

profile of v3, /device:TPU:7, one launch (start us, length us, event | category | flops | bytes accessed | tf_op | source)
XLA Modules:
  0.0 23.6 jit_solution(12637080352865881381)
XLA Ops:
  0.6 0.7 %collective-permute-start.1 = (s32[4,128]{1,0:T(4,128)}, s32[4,128]{1,0:T(4,128)S(1)}, u32[]{:S(2)}, u32[]{:S(2)}) collective-permute-start(s32[4,128]{1,0:T(4,128)} %cells.1), channel_id=1, source_target_pairs={{0,1},{1,0},{2,3},{3,2},{4,5},{5,4},{6,7},{7,6},{8,9},{9,8},{10,11... | collective-permute-start | bytes 6152 | tf_op jit(solution)/shard_map/ppermute | solution.py:38
  1.4 0.1 collective-permute-start
  1.4 1.0 %pack.1 = (f32[5,4,2048]{2,1,0:T(4,128)S(1)}, f32[2,128]{1,0:T(2,128)S(1)}) custom-call(f32[32,1920]{1,0:T(8,128)} %depth_in.1, f32[32,1920]{1,0:T(8,128)} %bed_in.1, s32[32,1920]{1,0:T(8,128)} %rough_in.1, f32[32,1920]{1,0:T(8,128)} %east_in.1, f32[32,1920]{1,0:T(8,128)} %south_in.1, f32[1,128]{1,0:T(1,128)} %bitcast.12, s32[4,128]{1,0:T(4,128)} %cells.1), custom_call_target="tpu_custom_call" | custom-call | tf_op jit(solution)/shard_map/pack/pallas_call | solution.py:552
  2.5 0.1 collective-permute-done
  2.6 0.0 collective-permute-done.1.cells.partner_cells
  2.6 3.3 %collective-permute-start.2 = (f32[5,4,2048]{2,1,0:T(4,128)S(1)}, f32[5,4,2048]{2,1,0:T(4,128)S(1)}, u32[]{:S(2)}, u32[]{:S(2)}) collective-permute-start(f32[5,4,2048]{2,1,0:T(4,128)S(1)} %join.1), channel_id=1, source_target_pairs={{1,2},{2,1},{3,4},{4,3},{5,6},{6,5},{7,8},{8,7},{9,10},{10,9},{11,... | collective-permute-start | bytes 491528 | tf_op jit(solution)/shard_map/ppermute | solution.py:38
  6.0 1.4 %load.1 = (f32[5,4,1920]{2,1,0:T(4,128)S(1)}, f32[40,1920]{1,0:T(8,128)S(1)}, f32[40,1920]{1,0:T(8,128)S(1)}, f32[40,1920]{1,0:T(8,128)S(1)}, f32[40,1920]{1,0:T(8,128)S(1)}, /*index=5*/s32[32,1920]{1,0:T(8,128)S(1)}) custom-call(f32[32,1920]{1,0:T(8,128)} %depth_in.1, f32[32,1920]{1,0:T(8,128)} %east_in.1, f32[32,1920]{1,0:T(8,128)} %south_in.1, ...), custom_call_target="tpu_custom_call" | custom-call | tf_op jit(solution)/shard_map/load/pallas_call | solution.py:581
  7.4 0.1 collective-permute-start.4
  7.5 0.0 copy-start
  7.5 0.6 %copy-done = f32[8]{0:T(128)S(1)} copy-done((f32[8]{0:T(128)S(1)}, f32[8]{0:T(128)}, u32[]{:S(2)}) %copy-start) | copy-done | bytes 56
  8.2 1.4 %prepare.1 = (f32[40,1920]{1,0:T(8,128)S(1)}, f32[40,1920]{1,0:T(8,128)S(1)}, f32[40,1920]{1,0:T(8,128)S(1)}, f32[40,1920]{1,0:T(8,128)S(1)}, f32[40,1920]{1,0:T...) custom-call(f32[8]{0:T(128)S(1)} %copy-done, ...), custom_call_target="tpu_custom_call", output_to_operand_aliasing={{0}: (5, {}), {1}: (6, {}), {2}: (7, {}), {3}: (8, {})} | custom-call | tf_op jit(solution)/shard_map/prepare/pallas_call | solution.py:591
  9.6 0.7 %collective-permute-done.2.by_other = f32[5,4,2048]{2,1,0:T(4,128)S(1)} collective-permute-done((f32[5,4,2048]{2,1,0:T(4,128)S(1)}, f32[5,4,2048]{2,1,0:T(4,128)S(1)}, u32[]{:S(2)}, u32[]{:S(2)}) %collective-permute-start.2) | collective-permute-done | bytes 163872 | tf_op jit(solution)/shard_map/ppermute | solution.py:38
  10.3 1.1 %collective-permute-start.3 = (f32[2,128]{1,0:T(2,128)S(1)}, f32[2,128]{1,0:T(2,128)S(1)}, u32[]{:S(2)}, u32[]{:S(2)}) collective-permute-start(f32[2,128]{1,0:T(2,128)S(1)} %relay.1), channel_id=1, source_target_pairs={{0,1},{1,0},{2,3},{3,2},{4,5},{5,4},{6,7},{7,6},{8,9},{9,8},{10,11... | collective-permute-start | bytes 3080 | tf_op jit(solution)/shard_map/ppermute | solution.py:38
  11.3 0.0 collective-permute-done.4.by_partner
  11.3 0.6 %border.1 = (f32[40,1920]{1,0:T(8,128)S(1)}, f32[40,1920]{1,0:T(8,128)S(1)}, f32[40,1920]{1,0:T(8,128)S(1)}, f32[40,1920]{1,0:T(8,128)S(1)}, f32[40,1920]{1,0:T(...) custom-call(f32[5,4,1920]{2,1,0:T(4,128)S(1)} %collective-permute-do, ...), custom_call_target="tpu_custom_call", output_to_operand_aliasing={{0}: (3, {}), {1}: (4, {}), {2}: (5, {}), {3}: (6, {}), {4}... | custom-call | tf_op jit(solution)/shard_map/border/pallas_call | solution.py:617
  11.9 0.3 %collective-permute-done.3.far = f32[2,128]{1,0:T(2,128)S(1)} collective-permute-done((f32[2,128]{1,0:T(2,128)S(1)}, f32[2,128]{1,0:T(2,128)S(1)}, u32[]{:S(2)}, u32[]{:S(2)}) %collective-permute-start.3) | collective-permute-done | bytes 1056 | tf_op jit(solution)/shard_map/ppermute | solution.py:38
  12.2 4.8 %steps.1 = (f32[1,128]{1,0:T(1,128)S(1)}, f32[1,128]{1,0:T(1,128)S(1)}, f32[1,128]{1,0:T(1,128)S(1)}, f32[40,1920]{1,0:T(8,128)S(1)}, f32[40,1920]{1,0:T(8,128)S...) custom-call(f32[2,128]{1,0:T(2,128)S(1)} %get-tuple-element.49.own, ...), custom_call_target="tpu_custom_call" | custom-call | tf_op jit(solution)/shard_map/steps/pallas_call | solution.py:628
  17.0 0.4 %collective-permute-start.5 = (f32[128]{0:T(128)S(1)}, f32[128]{0:T(128)S(1)}, u32[]{:S(2)}, u32[]{:S(2)}) collective-permute-start(f32[128]{0:T(128)S(1)} %bitcast.11), channel_id=1, source_target_pairs={{0,1},{1,0},{2,3},{3,2},{4,5},{5,4},{6,7},{7,6},{8,9},{9,8},{10,11... | collective-permute-start | bytes 1544 | tf_op jit(solution)/shard_map/ppermute | solution.py:38
  17.3 3.2 %collective-permute-start.6 = (f32[128]{0:T(128)S(1)}, f32[128]{0:T(128)S(1)}, u32[]{:S(2)}, u32[]{:S(2)}) collective-permute-start(f32[128]{0:T(128)S(1)} %bitcast.10), channel_id=1, source_target_pairs={{1,2},{2,1},{3,4},{4,3},{5,6},{6,5},{7,8},{8,7},{9,10},{10,9},{11,... | collective-permute-start | bytes 1544 | tf_op jit(solution)/shard_map/ppermute | solution.py:38
  20.5 1.6 %last.1 = (f32[32,1920]{1,0:T(8,128)}, f32[32,1920]{1,0:T(8,128)}, f32[32,1920]{1,0:T(8,128)}) custom-call(f32[40,1920]{1,0:T(8,128)S(1)} %get-tuple-element.82.refs_0_, f32[40,1920]{1,0:T(8,128)S(1)} %get-tuple-element.83.refs_1_, f32[40,1920]{1,0:T(8,128)S(1)} %get-tuple-element.84.refs_2_, f32[40,1920]{1,0:T(8,128)S(1)} %get-tuple-element.72.refs_3_, ...), custom_call_target="tpu_custom_call" | custom-call | tf_op jit(solution)/shard_map/last/pallas_call | solution.py:649
  22.1 0.0 collective-permute-done.5
  22.1 0.9 %collective-permute-done.6 = f32[128]{0:T(128)S(1)} collective-permute-done((f32[128]{0:T(128)S(1)}, f32[128]{0:T(128)S(1)}, u32[]{:S(2)}, u32[]{:S(2)}) %collective-permute-start.6) | collective-permute-done | bytes 544 | tf_op jit(solution)/shard_map/ppermute | solution.py:38
  23.1 0.5 %fusion = f32[128]{0:T(128)} fusion(f32[128]{0:T(128)S(1)} %collective-permute-done.6, f32[128]{0:T(128)S(1)} %collective-permute-done.5, f32[1,128]{1,0:T(1,128)S(1)} %get-tuple-element.91), kind=kLoop, calls=%fused_computation.1 | loop fusion | flops 256 | bytes 2048 | tf_op jit(solution)/shard_map/add | solution.py:659
  (2 shorter events, 0.0 us)
Async XLA Ops:
  0.6 2.0 %collective-permute-start.1 = (s32[4,128]{1,0:T(4,128)}, s32[4,128]{1,0:T(4,128)S(1)}, u32[]{:S(2)}, u32[]{:S(2)}) collective-permute-start(s32[4,128]{1,0:T(4,128)} %cells.1), channel_id=1, source_target_pairs={{0,1},{1,0},{2,3},{3,2},{4,5},{5,4},{6,7},{7,6},{8,9},{9,8},{10,11... | collective-permute-start | bytes 6152 | tf_op jit(solution)/shard_map/ppermute | solution.py:38
  1.4 1.3 %collective-permute-start = (f32[128]{0:T(128)}, f32[128]{0:T(128)S(1)}, u32[]{:S(2)}, u32[]{:S(2)}) collective-permute-start(f32[128]{0:T(128)} %param.11), channel_id=1, source_target_pairs={{0,1},{1,0},{2,3},{3,2},{4,5},{5,4},{6,7},{7,6},{8,9},{9,8},{10,11... | collective-permute-start | bytes 1544 | tf_op jit(solution)/shard_map/ppermute | solution.py:38
  2.6 7.6 %collective-permute-start.2 = (f32[5,4,2048]{2,1,0:T(4,128)S(1)}, f32[5,4,2048]{2,1,0:T(4,128)S(1)}, u32[]{:S(2)}, u32[]{:S(2)}) collective-permute-start(f32[5,4,2048]{2,1,0:T(4,128)S(1)} %join.1), channel_id=1, source_target_pairs={{1,2},{2,1},{3,4},{4,3},{5,6},{6,5},{7,8},{8,7},{9,10},{10,9},{11,... | collective-permute-start | bytes 491528 | tf_op jit(solution)/shard_map/ppermute | solution.py:38
  7.4 3.9 %collective-permute-start.4 = (f32[5,4,1920]{2,1,0:T(4,128)S(1)}, f32[5,4,1920]{2,1,0:T(4,128)S(1)}, u32[]{:S(2)}, u32[]{:S(2)}) collective-permute-start(f32[5,4,1920]{2,1,0:T(4,128)S(1)} %get-tuple-element.57), channel_id=1, source_target_pairs={{0,1},{1,0},{2,3},{3,2},{4,5},{5,4},{6,7},{7,6},{8,9},{9,8},{10,11... | collective-permute-start | bytes 460808 | tf_op jit(solution)/shard_map/ppermute | solution.py:38
  7.5 0.7 %copy-start = (f32[8]{0:T(128)S(1)}, f32[8]{0:T(128)}, u32[]{:S(2)}) copy-start(f32[8]{0:T(128)} %table.1) | copy-start | bytes 100
  10.3 1.9 %collective-permute-start.3 = (f32[2,128]{1,0:T(2,128)S(1)}, f32[2,128]{1,0:T(2,128)S(1)}, u32[]{:S(2)}, u32[]{:S(2)}) collective-permute-start(f32[2,128]{1,0:T(2,128)S(1)} %relay.1), channel_id=1, source_target_pairs={{0,1},{1,0},{2,3},{3,2},{4,5},{5,4},{6,7},{7,6},{8,9},{9,8},{10,11... | collective-permute-start | bytes 3080 | tf_op jit(solution)/shard_map/ppermute | solution.py:38
  17.0 5.2 %collective-permute-start.5 = (f32[128]{0:T(128)S(1)}, f32[128]{0:T(128)S(1)}, u32[]{:S(2)}, u32[]{:S(2)}) collective-permute-start(f32[128]{0:T(128)S(1)} %bitcast.11), channel_id=1, source_target_pairs={{0,1},{1,0},{2,3},{3,2},{4,5},{5,4},{6,7},{7,6},{8,9},{9,8},{10,11... | collective-permute-start | bytes 1544 | tf_op jit(solution)/shard_map/ppermute | solution.py:38
  17.3 5.7 %collective-permute-start.6 = (f32[128]{0:T(128)S(1)}, f32[128]{0:T(128)S(1)}, u32[]{:S(2)}, u32[]{:S(2)}) collective-permute-start(f32[128]{0:T(128)S(1)} %bitcast.10), channel_id=1, source_target_pairs={{1,2},{2,1},{3,4},{4,3},{5,6},{6,5},{7,8},{8,7},{9,10},{10,9},{11,... | collective-permute-start | bytes 1544 | tf_op jit(solution)/shard_map/ppermute | solution.py:38

commit v4 on v3

--- a/solution.py
+++ b/solution.py
@@ -346,13 +346,11 @@
         south[rows - 8 :, at] = jnp.where(kept, q0, new_south)
 
 
-def substep(fluxes_done, last, corridor, wall, refs):
+def substep(fluxes_done, tall, windows, corridor, wall, refs):
     surf, east, south, bed_e, bed_s, drag_e, drag_s, total, covers, count = refs
     ext, columns = surf.shape
-    rows = ext - 2 * HALO
     chunks = columns // LANES
-    tall = rows if last else ext
-    reach = 2 if last else corridor
+    reach = corridor if windows else 2
     lane = lanes_of(tall)
     zero = jnp.zeros((tall, LANES), jnp.float32)
 
@@ -375,7 +373,7 @@
             for by in range(reach - 1)
         ]
         if fluxes_done:
-            new_east, new_south = east[:, at], south[:, at]
+            new_east, new_south = east[:tall, at], south[:, at]
         else:
             new_east = face(
                 east[:tall, at], s0[:tall], moved[0], bed_e[:tall, at], drag_e[:tall, at]
@@ -388,9 +386,9 @@
         held = total[:tall, at]
         summed, state = right_sum(held, state)
         new_total = None
-        if not last:
-            window = (s0 + moved[0]) + sum(moved[2:], moved[1])
-            new_total = (1.0 - corridor * DRAIN) * held + count[:, at] * window
+        if windows:
+            window = (s0[:tall] + moved[0]) + sum(moved[2:], moved[1])
+            new_total = (1.0 - corridor * DRAIN) * held + count[:tall, at] * window
         east_rolled = pltpu.roll(new_east, 1, 1)
         north = pltpu.roll(new_south, 1, 0)
         inflow = jnp.where(lane < 1, east_last, east_rolled) + north[:tall]
@@ -402,67 +400,104 @@
         s0, rolled = s1, rolled_then
 
 
-def steps_kernel(corridor, tiles, own, far, *refs):
-    surf, east, south, bed_e, bed_s, drag_e, drag_s, number, total = refs[:9]
-    takes, at_lane, takes_near, at_lane_near = refs[9:13]
-    own_term, partner_term, other_term = refs[13:16]
-    surf_out, east_out, south_out, total_out, covers = refs[16:21]
-    count, total_0, total_1, total_2, surf_1, surf_2, east_1, south_1 = refs[21:]
+def first_kernel(corridor, surf, east, south, number, total, *refs):
+    surf_1, total_0, total_1, count, covers = refs
+    ext, columns = surf.shape
+    rows = ext - 2 * HALO
+    chunks = columns // LANES
+    zero = jnp.zeros((rows, LANES), jnp.float32)
+    state = (zero, zero)
+    for chunk in range(chunks):
+        at = cols(chunk)
+        starting = number[:rows, at]
+        count[:rows, at] = (FEED * DRAIN) * starting
+        total_0[:rows, at] = FEED * total[:rows, at]
+        summed, state = right_sum(starting, state)
+        covers[:rows, at] = FEED * summed
+    own = pl.ds(0, rows)
+    refs = (surf, east, south, None, None, None, None, total_0, covers, count)
+    for chunk, new_surf, _, _, new_total in substep(True, rows, True, corridor, None, refs):
+        surf_1[own, cols(chunk)] = new_surf
+        total_1[own, cols(chunk)] = new_total
+
+
+def second_kernel(corridor, tiles, far, surf, east, south, *refs):
+    bed_e, bed_s, drag_e, drag_s, number, total = refs[:6]
+    surf_1, total_1, count, covers = refs[10:14]
+    surf_2, east_2, south_2, total_2 = refs[14:18]
+    ext, columns = surf.shape
+    rows = ext - 2 * HALO
+    chunks = columns // LANES
+    position = lax.axis_index("gy")
+    tail = slice(rows, ext)
+
+    valid, node_row, node_chunk, node_lane = located(far[1:2, :], position, rows, ext, columns)
+    key = jnp.where(valid & (node_row >= rows), node_chunk * 8 + (node_row - rows), -1)
+    starts, levels = scattered(far[0:1, :], key, node_lane, chunks * 8)
+    zero = jnp.zeros((ext - rows, LANES), jnp.float32)
+    lane = lanes_of(ext - rows)
+    state, state_levels = (zero, zero), (zero, zero)
+    east_last = zero
+    for chunk in range(chunks):
+        at, mine = cols(chunk), slice(chunk * 8, chunk * 8 + 8)
+        then = cols(min(chunk + 1, chunks - 1))
+        starting = number[tail, at] + starts[mine]
+        held = FEED * (total[tail, at] + levels[mine])
+        starting_sum, state = right_sum(starting, state)
+        summed, state_levels = right_sum(held, state_levels)
+        s0 = surf[tail, at]
+        window = s0
+        for by in range(1, corridor):
+            window = window + moved_left(s0, surf[tail, then], by)
+        count_here = (FEED * DRAIN) * starting
+        covers_here = FEED * starting_sum
+        count[tail, at] = count_here
+        covers[tail, at] = covers_here
+        total_1[tail, at] = (1.0 - corridor * DRAIN) * held + count_here * window
+        new_east, new_south = east[tail, at], south[tail, at]
+        east_rolled = pltpu.roll(new_east, 1, 1)
+        north = pltpu.roll(south[rows - 8 :, at], 1, 0)[8:]
+        inflow = jnp.where(lane < 1, east_last, east_rolled) + north
+        east_last = east_rolled
+        gain = summed - covers_here * s0
+        surf_1[tail, at] = s0 + (SPREAD * (inflow - (new_east + new_south)) + gain)
+
+    refs = (surf_1, east, south, bed_e, bed_s, drag_e, drag_s, total_1, covers, count)
+    after = (surf_2, east_2, south_2, total_2)
+    steps = substep(False, ext, True, corridor, wall_of(ext, tiles), refs)
+    for chunk, *results in steps:
+        for target, result in zip(after, results):
+            target[:, cols(chunk)] = result
+
+
+def third_kernel(corridor, tiles, *refs):
+    after = refs[10:]
+    for chunk, *results in substep(
+        False, refs[0].shape[0], True, corridor, wall_of(refs[0].shape[0], tiles), refs[:10]
+    ):
+        for target, result in zip(after, results):
+            target[:, cols(chunk)] = result
+
+
+def terms_kernel(corridor, own, surf, total, total_0, count, *refs):
+    takes, at_lane, takes_near, at_lane_near, own_term, partner_term, other_term = refs
     ext, columns = surf.shape
     rows = ext - 2 * HALO
     owned = own.shape[1]
     chunks = columns // LANES
-    position = lax.axis_index("gy")
-
-    valid, node_row, node_chunk, node_lane = located(far[1:2, :], position, rows, ext, columns)
-    key = jnp.where(valid & (node_row >= rows), node_chunk * 8 + (node_row - rows), -1)
-    starts, levels = scattered(far[0:1, :], key, node_lane, chunks * 8)
-    zero = jnp.zeros((ext, LANES), jnp.float32)
-    state = (zero, zero)
-    for chunk in range(chunks):
-        at, mine = cols(chunk), slice(chunk * 8, chunk * 8 + 8)
-        starting = number[:, at]
-        starting = jnp.concatenate([starting[:rows], starting[rows:] + starts[mine]], axis=0)
-        held = total[:, at]
-        held = FEED * jnp.concatenate([held[:rows], held[rows:] + levels[mine]], axis=0)
-        count[:, at] = (FEED * DRAIN) * starting
-        total_0[:, at] = held
-        covering, state = right_sum(starting, state)
-        covers[:, at] = FEED * covering
-
-    wall = wall_of(ext, tiles)
-    faces = (bed_e, bed_s, drag_e, drag_s)
-    befores = (
-        (surf, east, south, total_0),
-        (surf_1, east, south, total_1),
-        (surf_2, east_1, south_1, total_2),
-    )
-    afters = (
-        (surf_1, None, None, total_1),
-        (surf_2, east_1, south_1, total_2),
-        (surf_out, east_out, south_out, total_out),
-    )
-    for step in range(STEPS - 1):
-        before, after = befores[step], afters[step]
-        state_refs = (*before[:3], *faces, before[3], covers, count)
-        for chunk, *results in substep(step == 0, False, corridor, wall, state_refs):
-            for target, result in zip(after, results):
-                if target is not None:
-                    target[:, cols(chunk)] = result
-
     kept = (1.0 - corridor * DRAIN) ** STEPS
     lane = lanes_of(rows)
 
     def turned(value):
         return [pltpu.roll(value, LANES - by, 1) for by in range(1, corridor)]
 
-    s0 = surf_out[:rows, cols(0)]
+    s0 = surf[:rows, cols(0)]
     rolled = turned(s0)
     levels = []
     for chunk in range(chunks):
         at = cols(chunk)
         if chunk + 1 < chunks:
-            s1 = surf_out[:rows, cols(chunk + 1)]
+            s1 = surf[:rows, cols(chunk + 1)]
             rolled_then = turned(s1)
         else:
             s1, rolled_then = s0, rolled
@@ -470,7 +505,7 @@
         for by in range(corridor - 1):
             window = window + jnp.where(lane >= LANES - 1 - by, rolled_then[by], rolled[by])
         starting = count[:rows, at]
-        held = (1.0 - corridor * DRAIN) * total_out[:rows, at] + starting * window
+        held = (1.0 - corridor * DRAIN) * total[:rows, at] + starting * window
         gained = held - kept * total_0[:rows, at]
         weight = jnp.maximum(starting * (1.0 / DRAIN), FEED)
         levels.append(gained * pl.reciprocal(weight, approx=True))
@@ -506,7 +541,7 @@
     chunks = columns // LANES
     group = 5
     copies = []
-    steps = substep(False, True, corridor, wall_of(ext, tiles), refs[:9] + (None,))
+    steps = substep(False, rows, False, corridor, wall_of(ext, tiles), refs[:9] + (None,))
     for chunk, new_surf, new_east, new_south, _ in steps:
         at = cols(chunk)
         results[0][:, at] = new_surf - bed[:rows, at]
@@ -625,24 +660,55 @@
         name="border",
     )(*[held(value) for value in (by_partner, by_other, table_rows, *fields)])
     surf, east, south, bed, _, *faces, number, total = fields
-    stepped = pl.pallas_call(
-        functools.partial(steps_kernel, corridor, tiles),
-        out_shape=[term] * 3 + [field] * 5,
-        in_specs=[VMEM_SPEC] * 15,
+    surf_1, total_0, total_1, count, covers = pl.pallas_call(
+        functools.partial(first_kernel, corridor),
+        out_shape=[field] * 5,
+        in_specs=[VMEM_SPEC] * 5,
+        out_specs=[VMEM_SPEC] * 5,
+        compiler_params=params,
+        name="first",
+    )(*[held(value) for value in (surf, east, south, number, total)])
+    surf_1, total_1, count, covers, surf_2, east_2, south_2, total_2 = pl.pallas_call(
+        functools.partial(second_kernel, corridor, tiles),
+        out_shape=[field] * 8,
+        in_specs=[VMEM_SPEC] * 14,
         out_specs=[VMEM_SPEC] * 8,
-        scratch_shapes=[field] * 8,
-        compiler_params=params,
-        name="steps",
+        input_output_aliases={10 + slot: slot for slot in range(4)},
+        compiler_params=params,
+        name="second",
     )(
         *[
             held(value)
             for value in (
-                *(own, from_far, surf, east, south, *faces, number, total),
+                *(from_far, surf, east, south, *faces, number, total),
+                *(surf_1, total_1, count, covers),
+            )
+        ]
+    )
+    surf, east, south, total = pl.pallas_call(
+        functools.partial(third_kernel, corridor, tiles),
+        out_shape=[field] * 4,
+        in_specs=[VMEM_SPEC] * 10,
+        out_specs=[VMEM_SPEC] * 4,
+        compiler_params=params,
+        name="third",
+    )(*[held(value) for value in (surf_2, east_2, south_2, *faces, total_2, covers, count)])
+    stepped = pl.pallas_call(
+        functools.partial(terms_kernel, corridor),
+        out_shape=[term] * 3,
+        in_specs=[VMEM_SPEC] * 9,
+        out_specs=[VMEM_SPEC] * 3,
+        compiler_params=params,
+        name="terms",
+    )(
+        *[
+            held(value)
+            for value in (
+                *(own, surf, total, total_0, count),
                 *(takes, at_lane, takes_near, at_lane_near),
             )
         ]
     )
-    surf, east, south, total, covers = stepped[3:]
     from_other = swapped(stepped[2].reshape(owned), 1)
     from_partner = swapped(stepped[1].reshape(owned), 0)
     result = pltpu.HBM((rows, columns), jnp.float32)

time: 23.8 us -> 24.2 us (1.017); the launches traced: 23.6 us -> 23.7 us
  Pallas kernels: 10.8 us -> 11.5 us
  starting transfers between devices: 8.87 us -> 8.57 us
    pallas_call x1 -> x4, Pallas kernels: 4.8 us -> 5.46 us  [the longest x1 1.77 us: local(): pl.pallas_call(functools.partial(first_kernel, corridor), out_shape=[fiel...]
    ppermute x7, starting transfers between devices: 8.87 us -> 8.57 us  [swapped(): return lax.ppermute(value, 'gy', pairs)]
    ppermute x7, waiting for transfers between devices: 2.02 us -> 1.78 us  [swapped(): return lax.ppermute(value, 'gy', pairs)]
  transfers between devices with their start and end apart: 7 -> 7, of which waited for: 4 -> 3; matrix products, arithmetic and copies ran while one was open for 0% -> 0% of each run, Pallas kernels for 25% -> 33%
where the time goes in v4:
time: 24.2 us; the launch traced here: 23.7 us
  Pallas kernels  11.5 us (48%)
  starting transfers between devices  8.57 us (35%)
  waiting for transfers between devices  1.78 us (7%)
  between operations  0.74 us (3%)
  local copies, waits for them, and re-layouts  0.65 us (3%)
  other arithmetic  0.51 us (2%)
    ppermute x7, starting transfers between devices, swapped(): return lax.ppermute(value, 'gy', pairs)  8.57 us
    ppermute x7, waiting for transfers between devices, swapped(): return lax.ppermute(value, 'gy', pairs)  1.78 us
    pallas_call x1, Pallas kernels, local(): pl.pallas_call(functools.partial(first_kernel, corridor), out_shape=[fiel...  1.77 us
    pallas_call x1, Pallas kernels, local(): pl.pallas_call(functools.partial(second_kernel, corridor, tiles), out_sha...  1.68 us
    pallas_call x1, Pallas kernels, local(): pl.pallas_call(functools.partial(last_kernel, corridor, tiles), out_shape...  1.59 us
    pallas_call x1, Pallas kernels, local(): pl.pallas_call(load_kernel, out_shape=[halo] + [field] * 4 + [pltpu.VMEM(...  1.44 us
    pallas_call x1, Pallas kernels, local(): pl.pallas_call(prepare_kernel, out_shape=[field] * 11 + [pltpu.VMEM((mann...  1.38 us
    pallas_call x1, Pallas kernels, local(): pl.pallas_call(functools.partial(third_kernel, corridor, tiles), out_shap...  1.35 us
  transfers between devices with their start and end apart: 7, of which 3 were waited for; matrix products, arithmetic and copies ran while one was open for 0% of the time, Pallas kernels for 33%

profile of v4, /device:TPU:7, one launch (start us, length us, event | category | flops | bytes accessed | tf_op | source)
XLA Modules:
  0.0 23.7 jit_solution(12944739442940353126)
XLA Ops:
  0.6 0.7 %collective-permute-start.1 = (s32[4,128]{1,0:T(4,128)}, s32[4,128]{1,0:T(4,128)S(1)}, u32[]{:S(2)}, u32[]{:S(2)}) collective-permute-start(s32[4,128]{1,0:T(4,128)} %cells.1), channel_id=1, source_target_pairs={{0,1},{1,0},{2,3},{3,2},{4,5},{5,4},{6,7},{7,6},{8,9},{9,8},{10,11... | collective-permute-start | bytes 6152 | tf_op jit(solution)/shard_map/ppermute | solution.py:38
  1.4 0.1 collective-permute-start
  1.4 1.0 %pack.1 = (f32[5,4,2048]{2,1,0:T(4,128)S(1)}, f32[2,128]{1,0:T(2,128)S(1)}) custom-call(f32[32,1920]{1,0:T(8,128)} %depth_in.1, f32[32,1920]{1,0:T(8,128)} %bed_in.1, s32[32,1920]{1,0:T(8,128)} %rough_in.1, f32[32,1920]{1,0:T(8,128)} %east_in.1, f32[32,1920]{1,0:T(8,128)} %south_in.1, f32[1,128]{1,0:T(1,128)} %bitcast.12, s32[4,128]{1,0:T(4,128)} %cells.1), custom_call_target="tpu_custom_call" | custom-call | tf_op jit(solution)/shard_map/pack/pallas_call | solution.py:587
  2.5 0.1 collective-permute-done
  2.6 0.0 collective-permute-done.1.cells.partner_cells
  2.6 3.3 %collective-permute-start.2 = (f32[5,4,2048]{2,1,0:T(4,128)S(1)}, f32[5,4,2048]{2,1,0:T(4,128)S(1)}, u32[]{:S(2)}, u32[]{:S(2)}) collective-permute-start(f32[5,4,2048]{2,1,0:T(4,128)S(1)} %join.1), channel_id=1, source_target_pairs={{1,2},{2,1},{3,4},{4,3},{5,6},{6,5},{7,8},{8,7},{9,10},{10,9},{11,... | collective-permute-start | bytes 491528 | tf_op jit(solution)/shard_map/ppermute | solution.py:38
  6.0 1.4 %load.1 = (f32[5,4,1920]{2,1,0:T(4,128)S(1)}, f32[40,1920]{1,0:T(8,128)S(1)}, f32[40,1920]{1,0:T(8,128)S(1)}, f32[40,1920]{1,0:T(8,128)S(1)}, f32[40,1920]{1,0:T(8,128)S(1)}, /*index=5*/s32[32,1920]{1,0:T(8,128)S(1)}) custom-call(f32[32,1920]{1,0:T(8,128)} %depth_in.1, f32[32,1920]{1,0:T(8,128)} %east_in.1, f32[32,1920]{1,0:T(8,128)} %south_in.1, ...), custom_call_target="tpu_custom_call" | custom-call | tf_op jit(solution)/shard_map/load/pallas_call | solution.py:616
  7.4 0.1 collective-permute-start.4
  7.5 0.0 copy-start
  7.5 0.6 %copy-done = f32[8]{0:T(128)S(1)} copy-done((f32[8]{0:T(128)S(1)}, f32[8]{0:T(128)}, u32[]{:S(2)}) %copy-start) | copy-done | bytes 56
  8.2 1.4 %prepare.1 = (f32[40,1920]{1,0:T(8,128)S(1)}, f32[40,1920]{1,0:T(8,128)S(1)}, f32[40,1920]{1,0:T(8,128)S(1)}, f32[40,1920]{1,0:T(8,128)S(1)}, f32[40,1920]{1,0:T...) custom-call(f32[8]{0:T(128)S(1)} %copy-done, ...), custom_call_target="tpu_custom_call", output_to_operand_aliasing={{0}: (5, {}), {1}: (6, {}), {2}: (7, {}), {3}: (8, {})} | custom-call | tf_op jit(solution)/shard_map/prepare/pallas_call | solution.py:626
  9.6 0.7 %collective-permute-done.2.by_other = f32[5,4,2048]{2,1,0:T(4,128)S(1)} collective-permute-done((f32[5,4,2048]{2,1,0:T(4,128)S(1)}, f32[5,4,2048]{2,1,0:T(4,128)S(1)}, u32[]{:S(2)}, u32[]{:S(2)}) %collective-permute-start.2) | collective-permute-done | bytes 163872 | tf_op jit(solution)/shard_map/ppermute | solution.py:38
  10.3 1.1 %collective-permute-start.3 = (f32[2,128]{1,0:T(2,128)S(1)}, f32[2,128]{1,0:T(2,128)S(1)}, u32[]{:S(2)}, u32[]{:S(2)}) collective-permute-start(f32[2,128]{1,0:T(2,128)S(1)} %relay.1), channel_id=1, source_target_pairs={{0,1},{1,0},{2,3},{3,2},{4,5},{5,4},{6,7},{7,6},{8,9},{9,8},{10,11... | collective-permute-start | bytes 3080 | tf_op jit(solution)/shard_map/ppermute | solution.py:38
  11.3 0.0 collective-permute-done.4.by_partner
  11.3 0.5 %border.1 = (f32[40,1920]{1,0:T(8,128)S(1)}, f32[40,1920]{1,0:T(8,128)S(1)}, f32[40,1920]{1,0:T(8,128)S(1)}, f32[40,1920]{1,0:T(8,128)S(1)}, f32[40,1920]{1,0:T(...) custom-call(f32[5,4,1920]{2,1,0:T(4,128)S(1)} %collective-permute-do, ...), custom_call_target="tpu_custom_call", output_to_operand_aliasing={{0}: (3, {}), {1}: (4, {}), {2}: (5, {}), {3}: (6, {}), {4}... | custom-call | tf_op jit(solution)/shard_map/border/pallas_call | solution.py:652
  11.9 1.8 %first.1 = (f32[40,1920]{1,0:T(8,128)S(1)}, f32[40,1920]{1,0:T(8,128)S(1)}, f32[40,1920]{1,0:T(8,128)S(1)}, f32[40,1920]{1,0:T(8,128)S(1)}, f32[40,1920]{1,0:T(8,128)S(1)}) custom-call(f32[40,1920]{1,0:T(8,128)S(1)} %get-tuple-element.79.surf, f32[40,1920]{1,0:T(8,128)S(1)} %get-tuple-element.80.east, f32[40,1920]{1,0:T(8,128)S(1)} %get-tuple-element.81.south, ...), custom_call_target="tpu_custom_call" | custom-call | tf_op jit(solution)/shard_map/first/pallas_call | solution.py:663
  13.7 0.0 collective-permute-done.3.far
  13.7 1.7 %second.1 = (f32[40,1920]{1,0:T(8,128)S(1)}, f32[40,1920]{1,0:T(8,128)S(1)}, f32[40,1920]{1,0:T(8,128)S(1)}, f32[40,1920]{1,0:T(8,128)S(1)}, f32[40,1920]{1,0:T(...) custom-call(f32[2,128]{1,0:T(2,128)S(1)} %collective-permute-done.3., ...), custom_call_target="tpu_custom_call", output_to_operand_aliasing={{0}: (10, {}), {1}: (11, {}), {2}: (12, {}), {3}: (13, {})} | custom-call | tf_op jit(solution)/shard_map/second/pallas_call | solution.py:671
  15.4 1.4 %third.1 = (f32[40,1920]{1,0:T(8,128)S(1)}, f32[40,1920]{1,0:T(8,128)S(1)}, f32[40,1920]{1,0:T(8,128)S(1)}, f32[40,1920]{1,0:T(8,128)S(1)}) custom-call(f32[40,1920]{1,0:T(8,128)S(1)} %get-tuple-element.92.refs_0_, f32[40,1920]{1,0:T(8,128)S(1)} %get-tuple-element.93.refs_1_, f32[40,1920]{1,0:T(8,128)S(1)} %get-tuple-element.94.refs_2_, ...), custom_call_target="tpu_custom_call" | custom-call | tf_op jit(solution)/shard_map/third/pallas_call | solution.py:688
  16.7 0.7 %terms.1 = (f32[1,128]{1,0:T(1,128)S(1)}, f32[1,128]{1,0:T(1,128)S(1)}, f32[1,128]{1,0:T(1,128)S(1)}) custom-call(f32[2,128]{1,0:T(2,128)S(1)} %get-tuple-element.61.own, f32[40,1920]{1,0:T(8,128)S(1)} %get-tuple-element.98.refs_0_.surf, f32[40,1920]{1,0:T(8,128)S(1)} %get-tuple-element.101.refs_7_.total, f32[40,1920]{1,0:T(8,128)S(1)} %get-tuple-element.106.total_0, ...), custom_call_target="tpu_custom_call" | custom-call | tf_op jit(solution)/shard_map/terms/pallas_call | solution.py:696
  17.4 0.1 collective-permute-start.5
  17.4 3.2 %collective-permute-start.6 = (f32[128]{0:T(128)S(1)}, f32[128]{0:T(128)S(1)}, u32[]{:S(2)}, u32[]{:S(2)}) collective-permute-start(f32[128]{0:T(128)S(1)} %bitcast.10), channel_id=1, source_target_pairs={{1,2},{2,1},{3,4},{4,3},{5,6},{6,5},{7,8},{8,7},{9,10},{10,9},{11,... | collective-permute-start | bytes 1544 | tf_op jit(solution)/shard_map/ppermute | solution.py:38
  20.7 1.6 %last.1 = (f32[32,1920]{1,0:T(8,128)}, f32[32,1920]{1,0:T(8,128)}, f32[32,1920]{1,0:T(8,128)}) custom-call(f32[40,1920]{1,0:T(8,128)S(1)} %get-tuple-element.98.refs_0_.surf, f32[40,1920]{1,0:T(8,128)S(1)} %get-tuple-element.99.refs_1_, f32[40,1920]{1,0:T(8,128)S(1)} %get-tuple-element.100.refs_2_, f32[40,1920]{1,0:T(8,128)S(1)} %get-tuple-element.82.refs_0_.refs_3_, ...), custom_call_target="tpu_custom_call" | custom-call | tf_op jit(solution)/shard_map/last/pallas_call | solution.py:715
  22.3 0.0 collective-permute-done.5
  22.3 0.9 %collective-permute-done.6 = f32[128]{0:T(128)S(1)} collective-permute-done((f32[128]{0:T(128)S(1)}, f32[128]{0:T(128)S(1)}, u32[]{:S(2)}, u32[]{:S(2)}) %collective-permute-start.6) | collective-permute-done | bytes 544 | tf_op jit(solution)/shard_map/ppermute | solution.py:38
  23.2 0.5 %fusion = f32[128]{0:T(128)} fusion(f32[128]{0:T(128)S(1)} %collective-permute-done.6, f32[128]{0:T(128)S(1)} %collective-permute-done.5, f32[1,128]{1,0:T(1,128)S(1)} %get-tuple-element.111), kind=kLoop, calls=%fused_computation.1 | loop fusion | flops 256 | bytes 2048 | tf_op jit(solution)/shard_map/add | solution.py:725
  (2 shorter events, 0.0 us)
Async XLA Ops:
  0.6 2.0 %collective-permute-start.1 = (s32[4,128]{1,0:T(4,128)}, s32[4,128]{1,0:T(4,128)S(1)}, u32[]{:S(2)}, u32[]{:S(2)}) collective-permute-start(s32[4,128]{1,0:T(4,128)} %cells.1), channel_id=1, source_target_pairs={{0,1},{1,0},{2,3},{3,2},{4,5},{5,4},{6,7},{7,6},{8,9},{9,8},{10,11... | collective-permute-start | bytes 6152 | tf_op jit(solution)/shard_map/ppermute | solution.py:38
  1.4 1.3 %collective-permute-start = (f32[128]{0:T(128)}, f32[128]{0:T(128)S(1)}, u32[]{:S(2)}, u32[]{:S(2)}) collective-permute-start(f32[128]{0:T(128)} %param.11), channel_id=1, source_target_pairs={{0,1},{1,0},{2,3},{3,2},{4,5},{5,4},{6,7},{7,6},{8,9},{9,8},{10,11... | collective-permute-start | bytes 1544 | tf_op jit(solution)/shard_map/ppermute | solution.py:38
  2.6 7.6 %collective-permute-start.2 = (f32[5,4,2048]{2,1,0:T(4,128)S(1)}, f32[5,4,2048]{2,1,0:T(4,128)S(1)}, u32[]{:S(2)}, u32[]{:S(2)}) collective-permute-start(f32[5,4,2048]{2,1,0:T(4,128)S(1)} %join.1), channel_id=1, source_target_pairs={{1,2},{2,1},{3,4},{4,3},{5,6},{6,5},{7,8},{8,7},{9,10},{10,9},{11,... | collective-permute-start | bytes 491528 | tf_op jit(solution)/shard_map/ppermute | solution.py:38
  7.4 3.9 %collective-permute-start.4 = (f32[5,4,1920]{2,1,0:T(4,128)S(1)}, f32[5,4,1920]{2,1,0:T(4,128)S(1)}, u32[]{:S(2)}, u32[]{:S(2)}) collective-permute-start(f32[5,4,1920]{2,1,0:T(4,128)S(1)} %get-tuple-element.67), channel_id=1, source_target_pairs={{0,1},{1,0},{2,3},{3,2},{4,5},{5,4},{6,7},{7,6},{8,9},{9,8},{10,11... | collective-permute-start | bytes 460808 | tf_op jit(solution)/shard_map/ppermute | solution.py:38
  7.5 0.7 %copy-start = (f32[8]{0:T(128)S(1)}, f32[8]{0:T(128)}, u32[]{:S(2)}) copy-start(f32[8]{0:T(128)} %table.1) | copy-start | bytes 100
  10.3 3.4 %collective-permute-start.3 = (f32[2,128]{1,0:T(2,128)S(1)}, f32[2,128]{1,0:T(2,128)S(1)}, u32[]{:S(2)}, u32[]{:S(2)}) collective-permute-start(f32[2,128]{1,0:T(2,128)S(1)} %relay.1), channel_id=1, source_target_pairs={{0,1},{1,0},{2,3},{3,2},{4,5},{5,4},{6,7},{7,6},{8,9},{9,8},{10,11... | collective-permute-start | bytes 3080 | tf_op jit(solution)/shard_map/ppermute | solution.py:38
  17.4 4.9 %collective-permute-start.5 = (f32[128]{0:T(128)S(1)}, f32[128]{0:T(128)S(1)}, u32[]{:S(2)}, u32[]{:S(2)}) collective-permute-start(f32[128]{0:T(128)S(1)} %bitcast.11), channel_id=1, source_target_pairs={{0,1},{1,0},{2,3},{3,2},{4,5},{5,4},{6,7},{7,6},{8,9},{9,8},{10,11... | collective-permute-start | bytes 1544 | tf_op jit(solution)/shard_map/ppermute | solution.py:38
  17.4 5.7 %collective-permute-start.6 = (f32[128]{0:T(128)S(1)}, f32[128]{0:T(128)S(1)}, u32[]{:S(2)}, u32[]{:S(2)}) collective-permute-start(f32[128]{0:T(128)S(1)} %bitcast.10), channel_id=1, source_target_pairs={{1,2},{2,1},{3,4},{4,3},{5,6},{6,5},{7,8},{8,7},{9,10},{10,9},{11,... | collective-permute-start | bytes 1544 | tf_op jit(solution)/shard_map/ppermute | solution.py:38

commit v5 on v4

--- a/solution.py
+++ b/solution.py
@@ -91,12 +91,34 @@
     return driven * pl.reciprocal(damping, approx=True)
 
 
-def right_sum(value, state):
-    lane = lanes_of(value.shape[0])
-    once = pltpu.roll(value, 1, 1)
-    pair = value + jnp.where(lane < 1, state[0], once)
-    twice = pltpu.roll(pair, 2, 1)
-    return pair + jnp.where(lane < 2, state[1], twice), (once, twice)
+def window_sums(blocks, reach, forward):
+    height = blocks[0].shape[0]
+    count = len(blocks)
+    spare = -(count * height) % 16
+    whole = blocks + ([jnp.zeros((spare, LANES), jnp.float32)] if spare else [])
+    whole = jnp.concatenate(whole, axis=0)
+    high = whole.astype(jnp.bfloat16)
+    low = (whole - high.astype(jnp.float32)).astype(jnp.bfloat16)
+    source = lax.broadcasted_iota(jnp.int32, (2 * LANES, 2 * LANES), 0) % LANES
+    target = lax.broadcasted_iota(jnp.int32, (2 * LANES, 2 * LANES), 1)
+    spill = target >= LANES
+    target = target % LANES
+    if forward:
+        ahead = source - target + jnp.where(spill, LANES, 0)
+    else:
+        ahead = target - source + jnp.where(spill, LANES, 0)
+    band = jnp.where((ahead >= 0) & (ahead < reach), 1.0, 0.0).astype(jnp.bfloat16)
+    sums = jnp.dot(
+        jnp.concatenate([high, low], axis=1), band, preferred_element_type=jnp.float32
+    )
+    results = []
+    for block in range(count):
+        result = sums[block * height : (block + 1) * height, :LANES]
+        beside = block + 1 if forward else block - 1
+        if 0 <= beside < count:
+            result = result + sums[beside * height : (beside + 1) * height, LANES:]
+        results.append(result)
+    return results
 
 
 def east_walled(value, chunk, chunks):
@@ -346,85 +368,80 @@
         south[rows - 8 :, at] = jnp.where(kept, q0, new_south)
 
 
-def substep(fluxes_done, tall, windows, corridor, wall, refs):
-    surf, east, south, bed_e, bed_s, drag_e, drag_s, total, covers, count = refs
+def fluxes(tall, wall, before, faces, after):
+    surf, east, south = before
+    bed_e, bed_s, drag_e, drag_s = faces
+    east_out, south_out = after
+    chunks = surf.shape[1] // LANES
+    for chunk in range(chunks):
+        at, then = cols(chunk), cols(min(chunk + 1, chunks - 1))
+        s0 = surf[:, at]
+        left = moved_left(s0[:tall], surf[:tall, then], 1)
+        new_east = face(east[:tall, at], s0[:tall], left, bed_e[:tall, at], drag_e[:tall, at])
+        east_out[:tall, at] = east_walled(new_east, chunk, chunks)
+        new_south = face(south[:, at], s0, moved_up(s0), bed_s[:, at], drag_s[:, at])
+        south_out[:, at] = jnp.concatenate(
+            [new_south[:-16], jnp.where(wall, 0.0, new_south[-16:])], axis=0
+        )
+
+
+def settled(mine, surf, east, south, gain):
     ext, columns = surf.shape
-    chunks = columns // LANES
-    reach = corridor if windows else 2
-    lane = lanes_of(tall)
-    zero = jnp.zeros((tall, LANES), jnp.float32)
-
-    def turned(value):
-        return [pltpu.roll(value[:tall], LANES - by, 1) for by in range(1, reach)]
-
-    s0 = surf[:, cols(0)]
-    rolled = turned(s0)
-    east_last = zero
-    state = (zero, zero)
-    for chunk in range(chunks):
-        at = cols(chunk)
-        if chunk + 1 < chunks:
-            s1 = surf[:, cols(chunk + 1)]
-            rolled_then = turned(s1)
+    for chunk in range(columns // LANES):
+        at = cols(chunk)
+        new_east = east[mine, at]
+        new_south = south[:, at]
+        lane = lanes_of(new_east.shape[0])
+        west = pltpu.roll(new_east, 1, 1)
+        if chunk > 0:
+            west = jnp.where(lane < 1, pltpu.roll(east[mine, cols(chunk - 1)], 1, 1), west)
         else:
-            s1, rolled_then = s0, rolled
-        moved = [
-            jnp.where(lane >= LANES - 1 - by, rolled_then[by], rolled[by])
-            for by in range(reach - 1)
-        ]
-        if fluxes_done:
-            new_east, new_south = east[:tall, at], south[:, at]
-        else:
-            new_east = face(
-                east[:tall, at], s0[:tall], moved[0], bed_e[:tall, at], drag_e[:tall, at]
-            )
-            new_east = east_walled(new_east, chunk, chunks)
-            new_south = face(south[:, at], s0, moved_up(s0), bed_s[:, at], drag_s[:, at])
-            new_south = jnp.concatenate(
-                [new_south[:-16], jnp.where(wall, 0.0, new_south[-16:])], axis=0
-            )
-        held = total[:tall, at]
-        summed, state = right_sum(held, state)
-        new_total = None
-        if windows:
-            window = (s0[:tall] + moved[0]) + sum(moved[2:], moved[1])
-            new_total = (1.0 - corridor * DRAIN) * held + count[:tall, at] * window
-        east_rolled = pltpu.roll(new_east, 1, 1)
-        north = pltpu.roll(new_south, 1, 0)
-        inflow = jnp.where(lane < 1, east_last, east_rolled) + north[:tall]
-        east_last = east_rolled
-        outflow = new_east + new_south[:tall]
-        gain = summed - covers[:tall, at] * s0[:tall]
-        new_surf = s0[:tall] + (SPREAD * (inflow - outflow) + gain)
-        yield chunk, new_surf, new_east, new_south, new_total
-        s0, rolled = s1, rolled_then
+            west = jnp.where(lane < 1, 0.0, west)
+        north = pltpu.roll(new_south, 1, 0)[mine]
+        inflow = west + north
+        s0 = surf[mine, at]
+        outflow = new_east + new_south[mine]
+        yield chunk, s0 + (SPREAD * (inflow - outflow) + gain(chunk, s0))
+
+
+def exchange(corridor, mine, surf, total, count, covers, total_out):
+    chunks = surf.shape[1] // LANES
+    windows = window_sums([surf[mine, cols(chunk)] for chunk in range(chunks)], corridor, True)
+    sums = window_sums([total[mine, cols(chunk)] for chunk in range(chunks)], corridor, False)
+    for chunk in range(chunks):
+        at = cols(chunk)
+        total_out[mine, at] = (1.0 - corridor * DRAIN) * total[mine, at] + count[
+            mine, at
+        ] * windows[chunk]
+
+    def gain(chunk, value):
+        return sums[chunk] - covers[mine, cols(chunk)] * value
+
+    return gain
 
 
 def first_kernel(corridor, surf, east, south, number, total, *refs):
     surf_1, total_0, total_1, count, covers = refs
-    ext, columns = surf.shape
-    rows = ext - 2 * HALO
-    chunks = columns // LANES
-    zero = jnp.zeros((rows, LANES), jnp.float32)
-    state = (zero, zero)
-    for chunk in range(chunks):
-        at = cols(chunk)
-        starting = number[:rows, at]
-        count[:rows, at] = (FEED * DRAIN) * starting
-        total_0[:rows, at] = FEED * total[:rows, at]
-        summed, state = right_sum(starting, state)
-        covers[:rows, at] = FEED * summed
-    own = pl.ds(0, rows)
-    refs = (surf, east, south, None, None, None, None, total_0, covers, count)
-    for chunk, new_surf, _, _, new_total in substep(True, rows, True, corridor, None, refs):
+    rows = surf.shape[0] - 2 * HALO
+    chunks = surf.shape[1] // LANES
+    own = slice(0, rows)
+    covering = window_sums([number[own, cols(chunk)] for chunk in range(chunks)], corridor, False)
+    for chunk in range(chunks):
+        at = cols(chunk)
+        count[own, at] = (FEED * DRAIN) * number[own, at]
+        covers[own, at] = FEED * covering[chunk]
+        total_0[own, at] = FEED * total[own, at]
+    gain = exchange(corridor, own, surf, total_0, count, covers, total_1)
+    for chunk, new_surf in settled(own, surf, east, south, gain):
         surf_1[own, cols(chunk)] = new_surf
-        total_1[own, cols(chunk)] = new_total
 
 
 def second_kernel(corridor, tiles, far, surf, east, south, *refs):
-    bed_e, bed_s, drag_e, drag_s, number, total = refs[:6]
+    faces = refs[:4]
+    number, total = refs[4:6]
     surf_1, total_1, count, covers = refs[10:14]
     surf_2, east_2, south_2, total_2 = refs[14:18]
+    total_0 = refs[18]
     ext, columns = surf.shape
     rows = ext - 2 * HALO
     chunks = columns // LANES
@@ -434,49 +451,35 @@
     valid, node_row, node_chunk, node_lane = located(far[1:2, :], position, rows, ext, columns)
     key = jnp.where(valid & (node_row >= rows), node_chunk * 8 + (node_row - rows), -1)
     starts, levels = scattered(far[0:1, :], key, node_lane, chunks * 8)
-    zero = jnp.zeros((ext - rows, LANES), jnp.float32)
-    lane = lanes_of(ext - rows)
-    state, state_levels = (zero, zero), (zero, zero)
-    east_last = zero
-    for chunk in range(chunks):
-        at, mine = cols(chunk), slice(chunk * 8, chunk * 8 + 8)
-        then = cols(min(chunk + 1, chunks - 1))
-        starting = number[tail, at] + starts[mine]
-        held = FEED * (total[tail, at] + levels[mine])
-        starting_sum, state = right_sum(starting, state)
-        summed, state_levels = right_sum(held, state_levels)
-        s0 = surf[tail, at]
-        window = s0
-        for by in range(1, corridor):
-            window = window + moved_left(s0, surf[tail, then], by)
-        count_here = (FEED * DRAIN) * starting
-        covers_here = FEED * starting_sum
-        count[tail, at] = count_here
-        covers[tail, at] = covers_here
-        total_1[tail, at] = (1.0 - corridor * DRAIN) * held + count_here * window
-        new_east, new_south = east[tail, at], south[tail, at]
-        east_rolled = pltpu.roll(new_east, 1, 1)
-        north = pltpu.roll(south[rows - 8 :, at], 1, 0)[8:]
-        inflow = jnp.where(lane < 1, east_last, east_rolled) + north
-        east_last = east_rolled
-        gain = summed - covers_here * s0
-        surf_1[tail, at] = s0 + (SPREAD * (inflow - (new_east + new_south)) + gain)
-
-    refs = (surf_1, east, south, bed_e, bed_s, drag_e, drag_s, total_1, covers, count)
-    after = (surf_2, east_2, south_2, total_2)
-    steps = substep(False, ext, True, corridor, wall_of(ext, tiles), refs)
-    for chunk, *results in steps:
-        for target, result in zip(after, results):
-            target[:, cols(chunk)] = result
-
-
-def third_kernel(corridor, tiles, *refs):
-    after = refs[10:]
-    for chunk, *results in substep(
-        False, refs[0].shape[0], True, corridor, wall_of(refs[0].shape[0], tiles), refs[:10]
-    ):
-        for target, result in zip(after, results):
-            target[:, cols(chunk)] = result
+    starting = [
+        number[tail, cols(chunk)] + starts[chunk * 8 : chunk * 8 + 8] for chunk in range(chunks)
+    ]
+    covering = window_sums(starting, corridor, False)
+    for chunk in range(chunks):
+        at = cols(chunk)
+        count[tail, at] = (FEED * DRAIN) * starting[chunk]
+        covers[tail, at] = FEED * covering[chunk]
+        total_0[tail, at] = FEED * (total[tail, at] + levels[chunk * 8 : chunk * 8 + 8])
+    gain = exchange(corridor, tail, surf, total_0, count, covers, total_1)
+    for chunk, new_surf in settled(tail, surf, east, south, gain):
+        surf_1[tail, cols(chunk)] = new_surf
+
+    every = slice(0, ext)
+    gain = exchange(corridor, every, surf_1, total_1, count, covers, total_2)
+    fluxes(ext, wall_of(ext, tiles), (surf_1, east, south), faces, (east_2, south_2))
+    for chunk, new_surf in settled(every, surf_1, east_2, south_2, gain):
+        surf_2[:, cols(chunk)] = new_surf
+
+
+def third_kernel(corridor, tiles, surf, east, south, *refs):
+    faces = refs[:4]
+    total, covers, count, surf_3, east_3, south_3, total_3 = refs[4:]
+    ext = surf.shape[0]
+    every = slice(0, ext)
+    gain = exchange(corridor, every, surf, total, count, covers, total_3)
+    fluxes(ext, wall_of(ext, tiles), (surf, east, south), faces, (east_3, south_3))
+    for chunk, new_surf in settled(every, surf, east_3, south_3, gain):
+        surf_3[:, cols(chunk)] = new_surf
 
 
 def terms_kernel(corridor, own, surf, total, total_0, count, *refs):
@@ -486,30 +489,15 @@
     owned = own.shape[1]
     chunks = columns // LANES
     kept = (1.0 - corridor * DRAIN) ** STEPS
-    lane = lanes_of(rows)
-
-    def turned(value):
-        return [pltpu.roll(value, LANES - by, 1) for by in range(1, corridor)]
-
-    s0 = surf[:rows, cols(0)]
-    rolled = turned(s0)
+    windows = window_sums([surf[:rows, cols(chunk)] for chunk in range(chunks)], corridor, True)
     levels = []
     for chunk in range(chunks):
         at = cols(chunk)
-        if chunk + 1 < chunks:
-            s1 = surf[:rows, cols(chunk + 1)]
-            rolled_then = turned(s1)
-        else:
-            s1, rolled_then = s0, rolled
-        window = s0
-        for by in range(corridor - 1):
-            window = window + jnp.where(lane >= LANES - 1 - by, rolled_then[by], rolled[by])
         starting = count[:rows, at]
-        held = (1.0 - corridor * DRAIN) * total[:rows, at] + starting * window
+        held = (1.0 - corridor * DRAIN) * total[:rows, at] + starting * windows[chunk]
         gained = held - kept * total_0[:rows, at]
         weight = jnp.maximum(starting * (1.0 / DRAIN), FEED)
         levels.append(gained * pl.reciprocal(weight, approx=True))
-        s0, rolled = s1, rolled_then
     spare = takes.shape[1] - chunks * rows
     if spare:
         levels.append(jnp.zeros((spare, LANES), jnp.float32))
@@ -531,31 +519,32 @@
     other_term[...] = terms[:, 2 * owned :]
 
 
-def last_kernel(corridor, tiles, *refs):
-    bed = refs[9]
-    targets = refs[10:13]
-    results = refs[13:16]
-    sems = refs[16]
-    ext, columns = bed.shape
+def last_kernel(corridor, tiles, surf, east, south, *refs):
+    faces = refs[:4]
+    total, covers, bed, depth_out, east_out, south_out = refs[4:10]
+    depth_new, east_new, south_new, sems = refs[10:]
+    ext, columns = surf.shape
     rows = ext - 2 * HALO
+    own = slice(0, rows)
+    copies = [
+        pltpu.make_async_copy(source.at[pl.ds(0, rows), :], target, sems.at[slot])
+        for slot, (source, target) in enumerate(
+            ((east_new, east_out), (south_new, south_out), (depth_new, depth_out))
+        )
+    ]
+    fluxes(rows, wall_of(ext, tiles), (surf, east, south), faces, (east_new, south_new))
+    copies[0].start()
+    copies[1].start()
     chunks = columns // LANES
-    group = 5
-    copies = []
-    steps = substep(False, rows, False, corridor, wall_of(ext, tiles), refs[:9] + (None,))
-    for chunk, new_surf, new_east, new_south, _ in steps:
-        at = cols(chunk)
-        results[0][:, at] = new_surf - bed[:rows, at]
-        results[1][:, at] = new_east
-        results[2][:, at] = new_south[:rows]
-        if (chunk + 1) % group == 0 or chunk + 1 == chunks:
-            first = chunk // group * group * LANES
-            width = pl.ds(first, (chunk + 1) * LANES - first)
-            for slot, (result, target) in enumerate(zip(results, targets)):
-                copy = pltpu.make_async_copy(
-                    result.at[:, width], target.at[:, width], sems.at[chunk // group, slot]
-                )
-                copy.start()
-                copies.append(copy)
+    sums = window_sums([total[own, cols(chunk)] for chunk in range(chunks)], corridor, False)
+
+    def gain(chunk, value):
+        return sums[chunk] - covers[own, cols(chunk)] * value
+
+    for chunk, new_surf in settled(own, surf, east_new, south_new, gain):
+        at = cols(chunk)
+        depth_new[:, at] = new_surf - bed[own, at]
+    copies[2].start()
     for copy in copies:
         copy.wait()
 
@@ -673,6 +662,7 @@
         out_shape=[field] * 8,
         in_specs=[VMEM_SPEC] * 14,
         out_specs=[VMEM_SPEC] * 8,
+        scratch_shapes=[field],
         input_output_aliases={10 + slot: slot for slot in range(4)},
         compiler_params=params,
         name="second",
@@ -717,8 +707,8 @@
         out_shape=[result] * 3,
         in_specs=[VMEM_SPEC] * 10,
         out_specs=[HBM_SPEC] * 3,
-        scratch_shapes=[pltpu.VMEM((rows, columns), jnp.float32)] * 3
-        + [pltpu.SemaphoreType.DMA((-(-chunks // 5), 3))],
+        scratch_shapes=[pltpu.VMEM((rows, columns), jnp.float32)] * 2
+        + [field, pltpu.SemaphoreType.DMA((3,))],
         compiler_params=params,
         name="last",
     )(*[held(value) for value in (surf, east, south, *faces, total, covers, bed)])

time: 24.2 us -> 21.8 us (0.901)
  Pallas kernels: 11.5 us -> 8.97 us
    pallas_call x1, Pallas kernels: 1.77 us -> 0.45 us  [local(): pl.pallas_call(functools.partial(first_kernel, corridor), out_shape=[fiel...]
    pallas_call x1, Pallas kernels: 1.68 us -> 1.12 us  [local(): pl.pallas_call(functools.partial(second_kernel, corridor, tiles), out_sha...]
    pallas_call x1, Pallas kernels: 1.35 us -> 0.86 us  [local(): pl.pallas_call(functools.partial(third_kernel, corridor, tiles), out_shap...]
  transfers between devices with their start and end apart: 7 -> 7, of which waited for: 3 -> 3; matrix products, arithmetic and copies ran while one was open for 0% -> 0% of each run, Pallas kernels for 33% -> 29%
where the time goes in v5:
time: 21.8 us; the launch traced here: 21.5 us
  Pallas kernels  8.97 us (41%)
  starting transfers between devices  8.67 us (40%)
  waiting for transfers between devices  1.99 us (9%)
  between operations  0.74 us (3%)
  local copies, waits for them, and re-layouts  0.65 us (3%)
  other arithmetic  0.51 us (2%)
    ppermute x7, starting transfers between devices, swapped(): return lax.ppermute(value, 'gy', pairs)  8.67 us
    ppermute x7, waiting for transfers between devices, swapped(): return lax.ppermute(value, 'gy', pairs)  1.99 us
    pallas_call x1, Pallas kernels, local(): pl.pallas_call(load_kernel, out_shape=[halo] + [field] * 4 + [pltpu.VMEM(...  1.44 us
    pallas_call x1, Pallas kernels, local(): pl.pallas_call(functools.partial(last_kernel, corridor, tiles), out_shape...  1.39 us
    pallas_call x1, Pallas kernels, local(): pl.pallas_call(prepare_kernel, out_shape=[field] * 11 + [pltpu.VMEM((mann...  1.38 us
    pallas_call x1, Pallas kernels, local(): pl.pallas_call(functools.partial(second_kernel, corridor, tiles), out_sha...  1.12 us
    pallas_call x1, Pallas kernels, local(): pl.pallas_call(pack_kernel, out_shape=[wide, pltpu.VMEM((2, owned), jnp.f...  1.02 us
    pallas_call x1, Pallas kernels, local(): pl.pallas_call(functools.partial(third_kernel, corridor, tiles), out_shap...  0.86 us
  transfers between devices with their start and end apart: 7, of which 3 were waited for; matrix products, arithmetic and copies ran while one was open for 0% of the time, Pallas kernels for 29%

profile of v5, /device:TPU:7, one launch (start us, length us, event | category | flops | bytes accessed | tf_op | source)
XLA Modules:
  0.0 21.5 jit_solution(6368223079621388197)
XLA Ops:
  0.6 0.7 %collective-permute-start.1 = (s32[4,128]{1,0:T(4,128)}, s32[4,128]{1,0:T(4,128)S(1)}, u32[]{:S(2)}, u32[]{:S(2)}) collective-permute-start(s32[4,128]{1,0:T(4,128)} %cells.1), channel_id=1, source_target_pairs={{0,1},{1,0},{2,3},{3,2},{4,5},{5,4},{6,7},{7,6},{8,9},{9,8},{10,11... | collective-permute-start | bytes 6152 | tf_op jit(solution)/shard_map/ppermute | solution.py:38
  1.4 0.1 collective-permute-start
  1.4 1.0 %pack.1 = (f32[5,4,2048]{2,1,0:T(4,128)S(1)}, f32[2,128]{1,0:T(2,128)S(1)}) custom-call(f32[32,1920]{1,0:T(8,128)} %depth_in.1, f32[32,1920]{1,0:T(8,128)} %bed_in.1, s32[32,1920]{1,0:T(8,128)} %rough_in.1, f32[32,1920]{1,0:T(8,128)} %east_in.1, f32[32,1920]{1,0:T(8,128)} %south_in.1, f32[1,128]{1,0:T(1,128)} %bitcast.12, s32[4,128]{1,0:T(4,128)} %cells.1), custom_call_target="tpu_custom_call" | custom-call | tf_op jit(solution)/shard_map/pack/pallas_call | solution.py:576
  2.5 0.1 collective-permute-done
  2.6 0.0 collective-permute-done.1.cells.partner_cells
  2.6 3.3 %collective-permute-start.2 = (f32[5,4,2048]{2,1,0:T(4,128)S(1)}, f32[5,4,2048]{2,1,0:T(4,128)S(1)}, u32[]{:S(2)}, u32[]{:S(2)}) collective-permute-start(f32[5,4,2048]{2,1,0:T(4,128)S(1)} %join.1), channel_id=1, source_target_pairs={{1,2},{2,1},{3,4},{4,3},{5,6},{6,5},{7,8},{8,7},{9,10},{10,9},{11,... | collective-permute-start | bytes 491528 | tf_op jit(solution)/shard_map/ppermute | solution.py:38
  6.0 1.4 %load.1 = (f32[5,4,1920]{2,1,0:T(4,128)S(1)}, f32[40,1920]{1,0:T(8,128)S(1)}, f32[40,1920]{1,0:T(8,128)S(1)}, f32[40,1920]{1,0:T(8,128)S(1)}, f32[40,1920]{1,0:T(8,128)S(1)}, /*index=5*/s32[32,1920]{1,0:T(8,128)S(1)}) custom-call(f32[32,1920]{1,0:T(8,128)} %depth_in.1, f32[32,1920]{1,0:T(8,128)} %east_in.1, f32[32,1920]{1,0:T(8,128)} %south_in.1, ...), custom_call_target="tpu_custom_call" | custom-call | tf_op jit(solution)/shard_map/load/pallas_call | solution.py:605
  7.4 0.1 collective-permute-start.4
  7.5 0.0 copy-start
  7.5 0.6 %copy-done = f32[8]{0:T(128)S(1)} copy-done((f32[8]{0:T(128)S(1)}, f32[8]{0:T(128)}, u32[]{:S(2)}) %copy-start) | copy-done | bytes 56
  8.2 1.4 %prepare.1 = (f32[40,1920]{1,0:T(8,128)S(1)}, f32[40,1920]{1,0:T(8,128)S(1)}, f32[40,1920]{1,0:T(8,128)S(1)}, f32[40,1920]{1,0:T(8,128)S(1)}, f32[40,1920]{1,0:T...) custom-call(f32[8]{0:T(128)S(1)} %copy-done, ...), custom_call_target="tpu_custom_call", output_to_operand_aliasing={{0}: (5, {}), {1}: (6, {}), {2}: (7, {}), {3}: (8, {})} | custom-call | tf_op jit(solution)/shard_map/prepare/pallas_call | solution.py:615
  9.6 0.7 %collective-permute-done.2.by_other = f32[5,4,2048]{2,1,0:T(4,128)S(1)} collective-permute-done((f32[5,4,2048]{2,1,0:T(4,128)S(1)}, f32[5,4,2048]{2,1,0:T(4,128)S(1)}, u32[]{:S(2)}, u32[]{:S(2)}) %collective-permute-start.2) | collective-permute-done | bytes 163872 | tf_op jit(solution)/shard_map/ppermute | solution.py:38
  10.3 1.1 %collective-permute-start.3 = (f32[2,128]{1,0:T(2,128)S(1)}, f32[2,128]{1,0:T(2,128)S(1)}, u32[]{:S(2)}, u32[]{:S(2)}) collective-permute-start(f32[2,128]{1,0:T(2,128)S(1)} %relay.1), channel_id=1, source_target_pairs={{0,1},{1,0},{2,3},{3,2},{4,5},{5,4},{6,7},{7,6},{8,9},{9,8},{10,11... | collective-permute-start | bytes 3080 | tf_op jit(solution)/shard_map/ppermute | solution.py:38
  11.3 0.0 collective-permute-done.4.by_partner
  11.3 0.5 %border.1 = (f32[40,1920]{1,0:T(8,128)S(1)}, f32[40,1920]{1,0:T(8,128)S(1)}, f32[40,1920]{1,0:T(8,128)S(1)}, f32[40,1920]{1,0:T(8,128)S(1)}, f32[40,1920]{1,0:T(...) custom-call(f32[5,4,1920]{2,1,0:T(4,128)S(1)} %collective-permute-do, ...), custom_call_target="tpu_custom_call", output_to_operand_aliasing={{0}: (3, {}), {1}: (4, {}), {2}: (5, {}), {3}: (6, {}), {4}... | custom-call | tf_op jit(solution)/shard_map/border/pallas_call | solution.py:641
  11.9 0.5 %first.1 = (f32[40,1920]{1,0:T(8,128)S(1)}, f32[40,1920]{1,0:T(8,128)S(1)}, f32[40,1920]{1,0:T(8,128)S(1)}, f32[40,1920]{1,0:T(8,128)S(1)}, f32[40,1920]{1,0:T(8,128)S(1)}) custom-call(f32[40,1920]{1,0:T(8,128)S(1)} %get-tuple-element.79.surf, f32[40,1920]{1,0:T(8,128)S(1)} %get-tuple-element.80.east, f32[40,1920]{1,0:T(8,128)S(1)} %get-tuple-element.81.south, ...), custom_call_target="tpu_custom_call" | custom-call | tf_op jit(solution)/shard_map/first/pallas_call | solution.py:652
  12.4 0.0 collective-permute-done.3.far
  12.4 1.1 %second.1 = (f32[40,1920]{1,0:T(8,128)S(1)}, f32[40,1920]{1,0:T(8,128)S(1)}, f32[40,1920]{1,0:T(8,128)S(1)}, f32[40,1920]{1,0:T(8,128)S(1)}, f32[40,1920]{1,0:T(...) custom-call(f32[2,128]{1,0:T(2,128)S(1)} %collective-permute-done.3., ...), custom_call_target="tpu_custom_call", output_to_operand_aliasing={{0}: (10, {}), {1}: (11, {}), {2}: (12, {}), {3}: (13, {})} | custom-call | tf_op jit(solution)/shard_map/second/pallas_call | solution.py:660
  13.5 0.9 %third.1 = (f32[40,1920]{1,0:T(8,128)S(1)}, f32[40,1920]{1,0:T(8,128)S(1)}, f32[40,1920]{1,0:T(8,128)S(1)}, f32[40,1920]{1,0:T(8,128)S(1)}) custom-call(f32[40,1920]{1,0:T(8,128)S(1)} %get-tuple-element.92.surf, f32[40,1920]{1,0:T(8,128)S(1)} %get-tuple-element.93.east, f32[40,1920]{1,0:T(8,128)S(1)} %get-tuple-element.94.south, ...), custom_call_target="tpu_custom_call" | custom-call | tf_op jit(solution)/shard_map/third/pallas_call | solution.py:678
  14.4 0.8 %terms.1 = (f32[1,128]{1,0:T(1,128)S(1)}, f32[1,128]{1,0:T(1,128)S(1)}, f32[1,128]{1,0:T(1,128)S(1)}) custom-call(f32[2,128]{1,0:T(2,128)S(1)} %get-tuple-element.61.own, f32[40,1920]{1,0:T(8,128)S(1)} %get-tuple-element.98.surf, f32[40,1920]{1,0:T(8,128)S(1)} %get-tuple-element.101.refs_4_.total, f32[40,1920]{1,0:T(8,128)S(1)} %get-tuple-element.106.total_0, ...), custom_call_target="tpu_custom_call" | custom-call | tf_op jit(solution)/shard_map/terms/pallas_call | solution.py:686
  15.1 0.2 collective-permute-start.5
  15.3 3.2 %collective-permute-start.6 = (f32[128]{0:T(128)S(1)}, f32[128]{0:T(128)S(1)}, u32[]{:S(2)}, u32[]{:S(2)}) collective-permute-start(f32[128]{0:T(128)S(1)} %bitcast.10), channel_id=1, source_target_pairs={{1,2},{2,1},{3,4},{4,3},{5,6},{6,5},{7,8},{8,7},{9,10},{10,9},{11,... | collective-permute-start | bytes 1544 | tf_op jit(solution)/shard_map/ppermute | solution.py:38
  18.5 1.4 %last.1 = (f32[32,1920]{1,0:T(8,128)}, f32[32,1920]{1,0:T(8,128)}, f32[32,1920]{1,0:T(8,128)}) custom-call(f32[40,1920]{1,0:T(8,128)S(1)} %get-tuple-element.98.surf, f32[40,1920]{1,0:T(8,128)S(1)} %get-tuple-element.99.east, f32[40,1920]{1,0:T(8,128)S(1)} %get-tuple-element.100.south, f32[40,1920]{1,0:T(8,128)S(1)} %get-tuple-element.82.refs_0_, ...), custom_call_target="tpu_custom_call" | custom-call | tf_op jit(solution)/shard_map/last/pallas_call | solution.py:705
  19.9 0.0 collective-permute-done.5
  19.9 1.1 %collective-permute-done.6 = f32[128]{0:T(128)S(1)} collective-permute-done((f32[128]{0:T(128)S(1)}, f32[128]{0:T(128)S(1)}, u32[]{:S(2)}, u32[]{:S(2)}) %collective-permute-start.6) | collective-permute-done | bytes 544 | tf_op jit(solution)/shard_map/ppermute | solution.py:38
  21.0 0.5 %fusion = f32[128]{0:T(128)} fusion(f32[128]{0:T(128)S(1)} %collective-permute-done.6, f32[128]{0:T(128)S(1)} %collective-permute-done.5, f32[1,128]{1,0:T(1,128)S(1)} %get-tuple-element.111), kind=kLoop, calls=%fused_computation.1 | loop fusion | flops 256 | bytes 2048 | tf_op jit(solution)/shard_map/add | solution.py:715
  (2 shorter events, 0.0 us)
Async XLA Ops:
  0.6 2.0 %collective-permute-start.1 = (s32[4,128]{1,0:T(4,128)}, s32[4,128]{1,0:T(4,128)S(1)}, u32[]{:S(2)}, u32[]{:S(2)}) collective-permute-start(s32[4,128]{1,0:T(4,128)} %cells.1), channel_id=1, source_target_pairs={{0,1},{1,0},{2,3},{3,2},{4,5},{5,4},{6,7},{7,6},{8,9},{9,8},{10,11... | collective-permute-start | bytes 6152 | tf_op jit(solution)/shard_map/ppermute | solution.py:38
  1.4 1.3 %collective-permute-start = (f32[128]{0:T(128)}, f32[128]{0:T(128)S(1)}, u32[]{:S(2)}, u32[]{:S(2)}) collective-permute-start(f32[128]{0:T(128)} %param.11), channel_id=1, source_target_pairs={{0,1},{1,0},{2,3},{3,2},{4,5},{5,4},{6,7},{7,6},{8,9},{9,8},{10,11... | collective-permute-start | bytes 1544 | tf_op jit(solution)/shard_map/ppermute | solution.py:38
  2.6 7.6 %collective-permute-start.2 = (f32[5,4,2048]{2,1,0:T(4,128)S(1)}, f32[5,4,2048]{2,1,0:T(4,128)S(1)}, u32[]{:S(2)}, u32[]{:S(2)}) collective-permute-start(f32[5,4,2048]{2,1,0:T(4,128)S(1)} %join.1), channel_id=1, source_target_pairs={{1,2},{2,1},{3,4},{4,3},{5,6},{6,5},{7,8},{8,7},{9,10},{10,9},{11,... | collective-permute-start | bytes 491528 | tf_op jit(solution)/shard_map/ppermute | solution.py:38
  7.4 3.9 %collective-permute-start.4 = (f32[5,4,1920]{2,1,0:T(4,128)S(1)}, f32[5,4,1920]{2,1,0:T(4,128)S(1)}, u32[]{:S(2)}, u32[]{:S(2)}) collective-permute-start(f32[5,4,1920]{2,1,0:T(4,128)S(1)} %get-tuple-element.67), channel_id=1, source_target_pairs={{0,1},{1,0},{2,3},{3,2},{4,5},{5,4},{6,7},{7,6},{8,9},{9,8},{10,11... | collective-permute-start | bytes 460808 | tf_op jit(solution)/shard_map/ppermute | solution.py:38
  7.5 0.7 %copy-start = (f32[8]{0:T(128)S(1)}, f32[8]{0:T(128)}, u32[]{:S(2)}) copy-start(f32[8]{0:T(128)} %table.1) | copy-start | bytes 100
  10.3 2.1 %collective-permute-start.3 = (f32[2,128]{1,0:T(2,128)S(1)}, f32[2,128]{1,0:T(2,128)S(1)}, u32[]{:S(2)}, u32[]{:S(2)}) collective-permute-start(f32[2,128]{1,0:T(2,128)S(1)} %relay.1), channel_id=1, source_target_pairs={{0,1},{1,0},{2,3},{3,2},{4,5},{5,4},{6,7},{7,6},{8,9},{9,8},{10,11... | collective-permute-start | bytes 3080 | tf_op jit(solution)/shard_map/ppermute | solution.py:38
  15.1 4.8 %collective-permute-start.5 = (f32[128]{0:T(128)S(1)}, f32[128]{0:T(128)S(1)}, u32[]{:S(2)}, u32[]{:S(2)}) collective-permute-start(f32[128]{0:T(128)S(1)} %bitcast.11), channel_id=1, source_target_pairs={{0,1},{1,0},{2,3},{3,2},{4,5},{5,4},{6,7},{7,6},{8,9},{9,8},{10,11... | collective-permute-start | bytes 1544 | tf_op jit(solution)/shard_map/ppermute | solution.py:38
  15.3 5.7 %collective-permute-start.6 = (f32[128]{0:T(128)S(1)}, f32[128]{0:T(128)S(1)}, u32[]{:S(2)}, u32[]{:S(2)}) collective-permute-start(f32[128]{0:T(128)S(1)} %bitcast.10), channel_id=1, source_target_pairs={{1,2},{2,1},{3,4},{4,3},{5,6},{6,5},{7,8},{8,7},{9,10},{10,9},{11,... | collective-permute-start | bytes 1544 | tf_op jit(solution)/shard_map/ppermute | solution.py:38
